TPU v7x, 32 devices: a whole 2x2x4 slice. The times are simulated.
32 devices in a mesh: dp: 8 (over z, core), pipe: 4 (over y, x).
Axes of the slice: x: 2, y: 2, z: 4, core: 2. Of those that a mesh axis runs over, the one named last changes fastest.
Arguments:
- acts_fwd: bfloat16 [4, 1024, 768], P('pipe', 'dp'), may hold values from -6 to 6
- acts_bwd: bfloat16 [4, 1024, 768], P('pipe', 'dp'), may hold values from -6 to 6
- cotangent: bfloat16 [4, 1024, 768], P('pipe', 'dp'), may hold values from -6 to 6
- lens_fwd: int32 [4, 8, 4], P('pipe', 'dp'), may hold values from 1 to 64, 128 in all within a row
- lens_bwd: int32 [4, 8, 4], P('pipe', 'dp'), may hold values from 1 to 64, 128 in all within a row
- w_proj: float32 [4, 768, 2048], P('pipe', 'dp'), may hold values from -0.21875 to 0.21875
- w_out: float32 [4, 512, 768], P('pipe', None, 'dp'), may hold values from -0.25 to 0.25
Outputs:
- next_acts: bfloat16 [4, 1024, 768], P('pipe', 'dp')
- prev_grads: bfloat16 [4, 1024, 768], P('pipe', 'dp')
- grad_proj: float32 [4, 768, 2048], P('pipe', 'dp')
- grad_out: float32 [4, 512, 768], P('pipe', None, 'dp')
Inputs may be any that keep to these rules, and one draw needn't show every extreme that they name: `lens_fwd`: each row of 4 lengths sums to 128; its largest is exactly 64. `lens_bwd`: each row of 4 lengths sums to 128; its largest is exactly 64.
All inputs are finite; a program needn't handle non-finite values.
Results may differ from a plain program's by a relative error of at most 0.011.
Values may be sent and summed in bfloat16 or wider, within the bound.
A program may use at most 64 MiB of HBM per device.

v0:
```python
import math

import jax
import jax.numpy as jnp
from jax import lax
from jax.sharding import PartitionSpec as P

HEADS = 4
HEAD_DIM = 128
HID = 512
LMAX = 64


EPS = 1e-05


def passed_along(array, axis, by):
    count = lax.axis_size(axis)
    return lax.ppermute(array, axis, [(i, (i + by) % count) for i in range(count)])


def jagged_mask(lengths, count):
    ends = jnp.cumsum(lengths)
    positions = jnp.arange(count, dtype=jnp.int32)
    segment = jnp.sum((positions[:, None] >= ends[None, :]).astype(jnp.int32), axis=1)
    keep = (segment[:, None] == segment[None, :]) & (positions[:, None] >= positions[None, :])
    return keep.astype(jnp.float32)


def layer_norm(values):
    center = values - jnp.mean(values, axis=-1, keepdims=True)
    inverse = lax.rsqrt(jnp.mean(center * center, axis=-1, keepdims=True) + EPS)
    return (center * inverse, inverse)


def norm_back(grad_normed, normed, inverse):
    return inverse * (
        grad_normed
        - jnp.mean(grad_normed, axis=-1, keepdims=True)
        - normed * jnp.mean(grad_normed * normed, axis=-1, keepdims=True)
    )


def silu_slope(values):
    sigma = jax.nn.sigmoid(values)
    return sigma * (1.0 + values * (1.0 - sigma))


def forward_parts(tokens, w_first, keep):
    count = tokens.shape[0]
    tok_float = tokens.astype(jnp.float32)
    normed, inverse = layer_norm(tok_float)
    normed_bf = normed.astype(jnp.bfloat16)
    preact = jnp.dot(normed_bf, w_first, preferred_element_type=jnp.float32)
    hidden = jax.nn.silu(preact).astype(jnp.bfloat16)
    gate_u = hidden[:, :HID]
    values_h = hidden[:, HID : 2 * HID].reshape(count, HEADS, HEAD_DIM)
    queries = hidden[:, 2 * HID : 3 * HID].reshape(count, HEADS, HEAD_DIM)
    keys_h = hidden[:, 3 * HID :].reshape(count, HEADS, HEAD_DIM)
    scores = jnp.einsum(
        "ihd,jhd->hij", queries, keys_h, preferred_element_type=jnp.float32
    ) * HEAD_DIM ** (-0.5)
    attn = (jax.nn.silu(scores) * keep[None] * (1.0 / LMAX)).astype(jnp.bfloat16)
    mixed = jnp.einsum("hij,jhd->ihd", attn, values_h, preferred_element_type=jnp.float32).reshape(
        count, HID
    )
    mixed_n, inverse_o = layer_norm(mixed)
    gated = (mixed_n * gate_u.astype(jnp.float32)).astype(jnp.bfloat16)
    return (
        tok_float,
        normed,
        inverse,
        normed_bf,
        preact,
        gate_u,
        values_h,
        queries,
        keys_h,
        scores,
        attn,
        mixed_n,
        inverse_o,
        gated,
    )


def forward(tokens, w_first, w_second, keep):
    parts = forward_parts(tokens, w_first, keep)
    return (parts[0] + jnp.dot(parts[13], w_second, preferred_element_type=jnp.float32)).astype(
        jnp.bfloat16
    )


def backward(tokens, cotan, w_first, w_second, keep):
    count = tokens.shape[0]
    (
        tok_float,
        normed,
        inverse,
        normed_bf,
        preact,
        gate_u,
        values_h,
        queries,
        keys_h,
        scores,
        attn,
        mixed_n,
        inverse_o,
        gated,
    ) = forward_parts(tokens, w_first, keep)
    grad_y = jnp.dot(cotan, w_second.T, preferred_element_type=jnp.float32)
    grad_u = grad_y * mixed_n
    grad_mn = grad_y * gate_u.astype(jnp.float32)
    grad_mixed = (
        norm_back(grad_mn, mixed_n, inverse_o).astype(jnp.bfloat16).reshape(count, HEADS, HEAD_DIM)
    )
    grad_attn = jnp.einsum("ihd,jhd->hij", grad_mixed, values_h, preferred_element_type=jnp.float32)
    grad_vals = jnp.einsum("hij,ihd->jhd", attn, grad_mixed, preferred_element_type=jnp.float32)
    grad_scores = (
        grad_attn * keep[None] * (1.0 / LMAX) * silu_slope(scores) * HEAD_DIM ** (-0.5)
    ).astype(jnp.bfloat16)
    grad_q = jnp.einsum("hij,jhd->ihd", grad_scores, keys_h, preferred_element_type=jnp.float32)
    grad_k = jnp.einsum("hij,ihd->jhd", grad_scores, queries, preferred_element_type=jnp.float32)
    grad_hidden = jnp.concatenate(
        [
            grad_u,
            grad_vals.reshape(count, HID),
            grad_q.reshape(count, HID),
            grad_k.reshape(count, HID),
        ],
        axis=1,
    )
    grad_pre = (grad_hidden * silu_slope(preact)).astype(jnp.bfloat16)
    grad_norm = jnp.dot(grad_pre, w_first.T, preferred_element_type=jnp.float32)
    grad_in = (cotan.astype(jnp.float32) + norm_back(grad_norm, normed, inverse)).astype(
        jnp.bfloat16
    )
    return (grad_in, normed_bf, grad_pre, gated)


def per_device(acts_fwd, acts_bwd, cotangent, lens_fwd, lens_bwd, w_proj, w_out):
    w_first, w_second = (
        lax.all_gather(w_proj[0].astype(jnp.bfloat16), "dp", axis=0, tiled=True),
        lax.all_gather(w_out[0].astype(jnp.bfloat16), "dp", axis=1, tiled=True),
    )
    block_rows = acts_fwd.shape[1]
    loss_scale = 1.0 / math.sqrt(lax.axis_size("dp") * block_rows)
    result = forward(acts_fwd[0], w_first, w_second, jagged_mask(lens_fwd[0, 0], block_rows))
    forward_out = passed_along(result, "pipe", 1)[None]
    cotan = cotangent[0]
    grad_in, normed_bf, grad_pre, gated = backward(
        acts_bwd[0], cotan, w_first, w_second, jagged_mask(lens_bwd[0, 0], block_rows)
    )
    term_proj = jnp.dot(normed_bf.T, grad_pre, preferred_element_type=jnp.float32) * loss_scale
    term_out = jnp.dot(gated.T, cotan, preferred_element_type=jnp.float32) * loss_scale
    summed_proj = lax.psum_scatter(term_proj, "dp", scatter_dimension=0, tiled=True)
    summed_out = lax.psum_scatter(term_out, "dp", scatter_dimension=1, tiled=True)
    arrived = passed_along(grad_in, "pipe", -1)
    return (forward_out, arrived[None], summed_proj[None], summed_out[None])


def solution(mesh):
    return jax.shard_map(
        per_device,
        mesh=mesh,
        in_specs=(
            P("pipe", "dp", None),
            P("pipe", "dp", None),
            P("pipe", "dp", None),
            P("pipe", "dp", None),
            P("pipe", "dp", None),
            P("pipe", "dp", None),
            P("pipe", None, "dp"),
        ),
        out_specs=(
            P("pipe", "dp", None),
            P("pipe", "dp", None),
            P("pipe", "dp", None),
            P("pipe", None, "dp"),
        ),
        check_vma=False,
    )
```

profile of v0, /device:TPU:0, one launch (start us, length us, event | category | flops | bytes accessed | tf_op | source)
XLA Modules:
  0.0 171.3 jit_solution(16387690853011293717)
XLA Ops:
  7.2 1.9 %convert_element_type.96 = bf16[1,96,2048]{2,1,0:T(8,128)(2,1)} convert(f32[1,96,2048]{2,1,0:T(8,128)} %param.12) | non-fusion elementwise | flops 196608 | bytes 1179648 | tf_op jit(solution)/shard_map/convert_element_type | solution.py:144
  9.2 0.8 reduce-window.17
  10.1 1.0 convert_reduce_fusion
  11.2 1.1 fusion.33
  12.4 38.8 %all-gather.4.cloned.1.call-done = bf16[1,768,2048]{2,1,0:T(8,128)(2,1)} async-done(((bf16[1,96,2048]{2,1,0:T(8,128)(2,1)}), bf16[1,768,2048]{2,1,0:T(8,128)(2,1)}) %all-gather.4.cloned.1.call-update) | async-done | bytes 3145744 | tf_op jit(solution)/shard_map/all_gather | solution.py:144
  51.2 2.7 %multiply_convert_fusion = (bf16[128,2048]{1,0:T(8,128)(2,1)S(1)}, f32[128,2048]{1,0:T(8,128)S(1)}) fusion(bf16[1,768,2048]{2,1,0:T(8,128)(2,1)} %all-gather.4.cloned.1.call-done, bf16[1,128,768]{2,1,0:T(8,128)(2,1)} %param.8, f32[128]{0:T(128)S(1)} %add_rsqrt_fusion.1, f32[128]{0:T(128)S(1)} %broadcast_multiply_fusion.6), kind=kOutput, calls=%fused_computation.19 | convolution fusion | flops 404357120 | bytes 4916224 | tf_op jit(solution)/shard_map/dot_general | solution.py:54
  54.3 0.2 convolution_multiply_fusion.3
  54.5 0.3 fusion.92
  55.1 1.6 convolution_multiply_fusion.1
  56.8 17.1 %all-gather.1 = bf16[1,512,768]{1,2,0:T(8,128)(2,1)S(1)} all-gather(bf16[1,512,96]{1,2,0:T(8,128)(2,1)S(1)} %convert_element_type.104), channel_id=3, replica_groups=mesh['dp'=8,'pipe'=4] {'dp'}, dimensions={2}, use_global_device_ids=true | all-gather | bytes 884736 | tf_op jit(solution)/shard_map/all_gather | solution.py:145
  74.0 0.4 fusion.76
  74.3 0.8 fusion.45
  75.2 0.2 fusion.48
  75.4 0.4 copy-done.6
  76.0 1.4 fusion.10
  77.3 0.2 fusion.93
  78.0 1.3 fusion.11
  79.3 3.7 %convolution_multiply_fusion = f32[768,2048]{1,0:T(8,128)} fusion(bf16[128,2048]{1,0:T(8,128)(2,1)S(1)} %fusion.11, bf16[1,128,768]{2,1,0:T(8,128)(2,1)S(1)} %copy-done, f32[128]{0:T(128)S(1)} %add_rsqrt_fusion.1, f32[128]{0:T(128)S(1)} %broadcast_multiply_fusion.6), kind=kOutput, calls=%fused_computation | convolution fusion | flops 404619264 | bytes 7013376 | tf_op jit(solution)/shard_map/dot_general | solution.py:155
  83.1 0.6 copy-done.9
  84.1 0.2 fusion.20
  84.4 2.6 %multiply_convert_fusion.1 = bf16[128,2048]{1,0:T(8,128)(2,1)S(1)} fusion(bf16[1,768,2048]{2,1,0:T(8,128)(2,1)} %all-gather.4.cloned.1.call-done, bf16[1,128,768]{2,1,0:T(8,128)(2,1)S(1)} %copy-done.1, f32[128]{0:T(128)S(1)} %add_rsqrt_fusion.3, f32[128]{0:T(128)S(1)} %broadcast_multiply_fusion.7), kind=kOutput, calls=%fused_computation.21 | convolution fusion | flops 404357120 | bytes 3867648 | tf_op jit(solution)/shard_map/dot_general | solution.py:54
  87.2 0.4 fusion.87
  87.9 0.4 fusion.6
  88.3 1.7 collective-permute-start
  90.0 3.2 %fusion.86 = (f32[128]{0:T(128)S(1)}, f32[128]{0:T(128)S(1)}, f32[128,768]{1,0:T(8,128)S(1)}) fusion(f32[128]{0:T(128)S(1)} %add_rsqrt_fusion.1, f32[128]{0:T(128)S(1)} %broadcast_multiply_fusion.6, bf16[1,128,768]{2,1,0:T(8,128)(2,1)S(1)} %copy-done, bf16[128,2048]{1,0:T(8,128)(2,1)S(1)} %fusion.11, bf16[1,768,2048]{2,1,0:T(8,128)(2,1)} %all-gather.4.cloned.1.call-done), kind=kOutput, calls=%fused_computation.121 | convolution fusion | flops 403242752 | bytes 4261888 | tf_op jit(solution)/shard_map/dot_general | solution.py:135
  93.2 0.2 fusion.32
  93.4 1.4 collective-permute-start.1
  94.8 1.6 collective-permute-done
  96.4 4.4 %collective-permute-done.1 = bf16[128,768]{1,0:T(8,128)(2,1)S(1)} collective-permute-done((bf16[128,768]{1,0:T(8,128)(2,1)S(1)}, bf16[128,768]{1,0:T(8,128)(2,1)S(1)}, u32[]{:S(2)}, u32[]{:S(2)}) %collective-permute-start.1) | collective-permute-done | bytes 196640 | tf_op jit(solution)/shard_map/ppermute | solution.py:19
  100.8 62.6 %reduce-scatter.3.cloned.1.call-done = f32[96,2048]{1,0:T(8,128)} async-done(((f32[768,2048]{1,0:T(8,128)}), f32[96,2048]{1,0:T(8,128)}) %reduce-scatter.3.cloned.1.call-update) | async-done | bytes 786448 | tf_op jit(solution)/shard_map/reduce_scatter | solution.py:157
  163.4 0.7 copy.89
  164.1 0.7 copy.90
  (56 shorter events, 2.4 us)
Async XLA Ops:
  7.2 44.1 %all-gather.4.cloned.1.call-start = ((), (), s32[]{:S(2)}) async-start(), calls=%async_computation.4 | async-start | bytes 3538944 | tf_op jit(solution)/shard_map/all_gather | solution.py:144
  9.2 91.6 %reduce-scatter.5.cloned.1.call-start = ((), (), s32[]{:S(2)}) async-start(), calls=%async_computation.3 | async-start | bytes 1769472 | tf_op jit(solution)/shard_map/reduce_scatter | solution.py:158
  12.4 42.1 %copy-start.7 = (f32[128,128]{1,0:T(8,128)}, f32[128,128]{1,0:T(8,128)S(1)}, u32[]{:S(2)}) copy-start(f32[128,128]{1,0:T(8,128)S(1)} %fusion.80) | copy-start | bytes 196612
  53.9 1.1 copy-start.2
  54.0 0.9 copy-start.5
  54.2 2.5 %copy-start.4 = (f32[1,512,96]{1,2,0:T(8,128)S(1)}, f32[1,512,96]{1,2,0:T(8,128)}, u32[]{:S(2)}) copy-start(f32[1,512,96]{1,2,0:T(8,128)} %param.13) | copy-start | bytes 589828
  54.5 20.9 %copy-start.3 = (f32[4,128,128]{2,1,0:T(8,128)}, f32[4,128,128]{2,1,0:T(8,128)S(1)}, u32[]{:S(2)}) copy-start(f32[4,128,128]{2,1,0:T(8,128)S(1)} %convolution_multiply_fusion.3) | copy-start | bytes 786436
  56.7 18.4 %copy-start.8 = (f32[128,128]{1,0:T(8,128)S(1)}, f32[128,128]{1,0:T(8,128)}, u32[]{:S(2)}) copy-start(f32[128,128]{1,0:T(8,128)} %copy-done.7) | copy-start | bytes 196612
  56.7 106.7 %reduce-scatter.3.cloned.1.call-start = ((), (), s32[]{:S(2)}) async-start(), calls=%async_computation.2 | async-start | bytes 7077888 | tf_op jit(solution)/shard_map/reduce_scatter | solution.py:157
  75.2 0.7 copy-start.6
  75.9 3.4 %copy-start = (bf16[1,128,768]{2,1,0:T(8,128)(2,1)S(1)}, bf16[1,128,768]{2,1,0:T(8,128)(2,1)}, u32[]{:S(2)}) copy-start(bf16[1,128,768]{2,1,0:T(8,128)(2,1)} %param.8) | copy-start | bytes 589828
  83.1 0.7 copy-start.9
  83.1 0.9 copy-start.1
  88.3 8.1 %collective-permute-start = (bf16[128,768]{1,0:T(8,128)(2,1)S(1)}, bf16[128,768]{1,0:T(8,128)(2,1)S(1)}, u32[]{:S(2)}, u32[]{:S(2)}) collective-permute-start(bf16[128,768]{1,0:T(8,128)(2,1)S(1)} %fusion.6), channel_id=1, source_target_pairs={{0,1},{1,2},{2,3},{3,0},{4,5},{5,6},{6,7},{7,4},{8,9},{9,10},{10,1... | collective-permute-start | bytes 589832 | tf_op jit(solution)/shard_map/ppermute | solution.py:19
  93.4 7.4 %collective-permute-start.1 = (bf16[128,768]{1,0:T(8,128)(2,1)S(1)}, bf16[128,768]{1,0:T(8,128)(2,1)S(1)}, u32[]{:S(2)}, u32[]{:S(2)}) collective-permute-start(bf16[128,768]{1,0:T(8,128)(2,1)S(1)} %fusion.32), channel_id=1, source_target_pairs={{0,3},{1,0},{2,1},{3,2},{4,7},{5,4},{6,5},{7,6},{8,11},{9,8},{10,9... | collective-permute-start | bytes 589832 | tf_op jit(solution)/shard_map/ppermute | solution.py:19
Sparse Core Ops, SparseCore 0:
  10.2 40.9 all-gather.3
  56.9 34.5 reduce-scatter.4
  94.3 69.0 reduce-scatter.2
where the time goes:
time: 172 us; the launch traced here: 171 us
  waiting for transfers between devices  107 us (62%)
  matrix products  17.5 us (10%)
  blocking collectives  17.1 us (10%)
  between operations  14.1 us (8%)
  other arithmetic  8.35 us (5%)
  local copies, waits for them, and re-layouts  3.51 us (2%)
  starting transfers between devices  3.16 us (2%)
    reduce_scatter x1, waiting for transfers between devices, per_device(): lax.psum_scatter(term_proj, 'dp', scatter_dimension=0, tiled=True)  62.6 us
    all_gather x1, waiting for transfers between devices, per_device(): lax.all_gather(w_proj[0].astype(jnp.bfloat16), 'dp', axis=0, tiled=True)  38.8 us
    all_gather x1, blocking collectives, per_device(): lax.all_gather(w_out[0].astype(jnp.bfloat16), 'dp', axis=1, tiled=True)  17.1 us
    ppermute x2, waiting for transfers between devices, passed_along(): lax.ppermute(array, axis, [(i, (i + by) % count) for i in range(count)])  6.01 us
    dot_general x2, matrix products, forward_parts(): preact = jnp.dot(normed_bf, w_first, preferred_element_type=jnp.float32)  5.3 us
    dot_general x1, matrix products, per_device(): jnp.dot(normed_bf.T, grad_pre, preferred_element_type=jnp.float32)  3.75 us
  transfers between devices with their start and end apart: 5, of which 4 were waited for; matrix products, arithmetic and copies ran while one was open for 11% of the time, Pallas kernels for 0%

commit v1 on v0

v1 whole, which is shorter than its diff:
```python
import functools
import math

import jax
import jax.numpy as jnp
from jax import lax
from jax.experimental import pallas as pl
from jax.experimental.pallas import tpu as pltpu
from jax.sharding import PartitionSpec as P

HEADS = 4
HEAD_DIM = 128
LMAX = 64
EPS = 1e-05
CORES = 2
MESH = pl.DeviceIdType.MESH
BF = jnp.bfloat16
F32 = jnp.float32

NN = (((1,), (0,)), ((), ()))
NT = (((1,), (1,)), ((), ()))
TN = (((0,), (0,)), ((), ()))


def dot(a, b, dims=NN):
    return lax.dot_general(a, b, dims, preferred_element_type=F32)


def sigmoid(v):
    return 0.5 + 0.5 * jnp.tanh(0.5 * v)


def layer_norm(values):
    center = values - jnp.mean(values, axis=-1, keepdims=True)
    inverse = lax.rsqrt(jnp.mean(center * center, axis=-1, keepdims=True) + EPS)
    return center * inverse, inverse


def norm_back(grad, normed, inverse):
    return inverse * (
        grad
        - jnp.mean(grad, axis=-1, keepdims=True)
        - normed * jnp.mean(grad * normed, axis=-1, keepdims=True)
    )


def jagged_mask(lens_ref, count):
    rows = lax.broadcasted_iota(jnp.int32, (count, count), 0)
    cols = lax.broadcasted_iota(jnp.int32, (count, count), 1)
    row_seg = jnp.zeros((count, count), jnp.int32)
    col_seg = jnp.zeros((count, count), jnp.int32)
    end = jnp.int32(0)
    for user in range(lens_ref.shape[2]):
        end = end + lens_ref[0, 0, user]
        row_seg += jnp.where(rows >= end, 1, 0)
        col_seg += jnp.where(cols >= end, 1, 0)
    keep = (row_seg == col_seg) & (cols <= rows)
    return jnp.where(keep, 1.0 / LMAX, 0.0)


def kernel(
    chips,
    phases,
    xf_ref,
    xb_ref,
    g_ref,
    lf_ref,
    lb_ref,
    w_ref,
    next_ref,
    prev_ref,
    gp_ref,
    go_ref,
    wall,
    xnf,
    xnb,
    normed_ref,
    norm_t,
    g_t,
    hidden,
    slope,
    gpre,
    gated_b,
    gnorm,
    fwd_out,
    bwd_out,
    own,
    psend,
    precv,
    lrecv,
    rrecv,
    stage,
    ag_right,
    ag_left,
    ag_part,
    ag_chain,
    ag_precv,
    rs_send,
    rs_part,
    rs_precv,
    rs_lrecv,
    rs_rrecv,
    pipe_sems,
):
    shard, wide = w_ref.shape
    count, model = xf_ref.shape[1:]
    hid = HEADS * HEAD_DIM
    proj = 4 * hid
    scale = HEAD_DIM ** (-0.5)
    loss_scale = 1.0 / math.sqrt(chips * CORES * count)
    me = lax.axis_index("dp")
    phase = lax.axis_index("pipe")
    z, c = lax.div(me, CORES), lax.rem(me, CORES)
    has_left, has_right = z > 0, z < chips - 1
    left, right, partner = {"dp": me - CORES}, {"dp": me + CORES}, {"dp": z * CORES + 1 - c}
    ahead = {"pipe": lax.rem(phase + 1, phases)}
    behind = {"pipe": lax.rem(phase + phases - 1, phases)}

    barrier = pltpu.get_barrier_semaphore()

    def greet(target):
        pl.semaphore_signal(barrier, inc=1, device_id=target, device_id_type=MESH)

    @pl.when(has_left)
    def _():
        greet(left)

    @pl.when(has_right)
    def _():
        greet(right)

    greet(partner)
    greet(ahead)
    greet(behind)

    def rows(chip, core):
        return pl.ds(pl.multiple_of((chip * CORES + core) * shard, shard), shard)

    wall[rows(z, c), :] = w_ref[...]

    neighbours = 3 + jnp.where(has_left, 1, 0) + jnp.where(has_right, 1, 0)
    pl.semaphore_wait(barrier, neighbours)

    def remote(src, dst, send_sem, recv_sem, target):
        return pltpu.make_async_remote_copy(
            src_ref=src,
            dst_ref=dst,
            send_sem=send_sem,
            recv_sem=recv_sem,
            device_id=target,
            device_id_type=MESH,
        )

    def gather(chip, core, send_sem, recv_sem, target):
        block = wall.at[rows(chip, core), :]
        return remote(block, block, send_sem.at[chip], recv_sem.at[chip], target)

    def to_right(chip):
        return gather(chip, c, ag_right, ag_chain, right)

    def to_left(chip):
        return gather(chip, c, ag_left, ag_chain, left)

    def to_partner(chip):
        return gather(chip, c, ag_part, ag_precv, partner)

    def from_partner(chip):
        return gather(chip, 1 - c, ag_part, ag_precv, partner)

    @pl.when(has_right)
    def _():
        to_right(z).start()

    @pl.when(has_left)
    def _():
        to_left(z).start()

    to_partner(z).start()

    normed_f, _ = layer_norm(xf_ref[0].astype(F32))
    xnf[...] = normed_f.astype(BF)
    normed_b, inverse_b = layer_norm(xb_ref[0].astype(F32))
    normed_ref[...] = normed_b
    xnb[...] = normed_b.astype(BF)
    norm_t[...] = normed_b.T.astype(BF)
    g_t[...] = g_ref[0].astype(F32).T.astype(BF)
    keep_b = jagged_mask(lb_ref, count)

    def gather_tick(t, carry):
        from_left, from_right = z - t, z + t

        @pl.when(from_left >= 0)
        def _():
            to_right(from_left).wait_recv()

            @pl.when(has_right)
            def _():
                to_right(from_left).start()

            to_partner(from_left).start()

        @pl.when(from_right < chips)
        def _():
            to_left(from_right).wait_recv()

            @pl.when(has_left)
            def _():
                to_left(from_right).start()

            to_partner(from_right).start()

        return carry

    lax.fori_loop(1, chips, gather_tick, 0)

    def partner_arrival(j, carry):
        from_partner(j).wait_recv()
        return carry

    lax.fori_loop(0, chips, partner_arrival, 0)

    tile = 256

    def project(x_ref, with_slope):
        def body(i, carry):
            cols = pl.ds(pl.multiple_of(i * tile, tile), tile)
            value = dot(x_ref[...], wall[:, cols])
            sigma = sigmoid(value)
            silu = value * sigma
            hidden[:, cols] = silu.astype(BF)
            if with_slope:
                slope[:, cols] = sigma + silu * (1.0 - sigma)
            return carry

        lax.fori_loop(0, proj // tile, body, 0)

    def part(which, head):
        start = which * hid + head * HEAD_DIM
        return hidden[:, start : start + HEAD_DIM]

    def attend(keep):
        sigmas, scores, attns, mixed = [], [], [], []
        for head in range(HEADS):
            score = dot(part(2, head), part(3, head), NT) * scale
            sigma = sigmoid(score)
            attn = (score * sigma * keep).astype(BF)
            mixed.append(dot(attn, part(1, head)))
            scores.append(score)
            sigmas.append(sigma)
            attns.append(attn)
        return sigmas, scores, attns, jnp.concatenate(mixed, axis=1)

    project(xnb, True)
    sigmas, scores, attns, mixed = attend(keep_b)
    mixed_n, inverse_o = layer_norm(mixed)
    gate = hidden[:, :hid].astype(F32)
    gated_b[...] = (mixed_n * gate).astype(BF)
    grad_y = dot(g_ref[0], wall[:, proj:])
    gpre[:, :hid] = (grad_y * mixed_n * slope[:, :hid]).astype(BF)
    grad_mixed = norm_back(grad_y * gate, mixed_n, inverse_o).astype(BF)
    for head in range(HEADS):
        grad_m = grad_mixed[:, head * HEAD_DIM : (head + 1) * HEAD_DIM]
        score, sigma = scores[head], sigmas[head]
        grad_attn = dot(grad_m, part(1, head), NT)
        grad_vals = dot(attns[head], grad_m, TN)
        grad_s = (
            grad_attn * keep_b * (sigma * (1.0 + score * (1.0 - sigma))) * scale
        ).astype(BF)
        grad_q = dot(grad_s, part(3, head))
        grad_k = dot(grad_s, part(2, head), TN)
        for which, grad in ((1, grad_vals), (2, grad_q), (3, grad_k)):
            start = which * hid + head * HEAD_DIM
            cols = slice(start, start + HEAD_DIM)
            gpre[:, cols] = (grad * slope[:, cols]).astype(BF)

    def part_copy(d):
        return remote(psend.at[d], precv.at[d], rs_part.at[d], rs_precv.at[d], partner)

    def right_copy(d):
        return remote(stage.at[d], lrecv.at[d], rs_send.at[d], rs_lrecv.at[d], right)

    def left_copy(d):
        return remote(stage.at[d], rrecv.at[d], rs_send.at[d], rs_rrecv.at[d], left)

    def term(k, carry):
        d = jnp.where(z < chips // 2, chips - 1 - k, k)
        other = rows(d, 1 - c)
        psend[d, :, :proj] = (dot(norm_t[other, :], gpre[...]) * loss_scale).astype(BF)
        psend[d, :, proj:] = (dot(g_t[other, :], gated_b[...]) * loss_scale).astype(BF)
        part_copy(d).start()
        mine = rows(d, c)
        own[d, :, :proj] = dot(norm_t[mine, :], gpre[...]) * loss_scale
        own[d, :, proj:] = dot(g_t[mine, :], gated_b[...]) * loss_scale
        return carry

    def chip_sum(d):
        part_copy(d).wait_recv()
        return own[d] + precv[d].astype(F32)

    def reduce_tick(tau, carry):
        @pl.when(has_right & (tau >= z))
        def _():
            d = chips - 1 - tau + z
            own[d] = chip_sum(d)

            @pl.when(has_left)
            def _():
                right_copy(d).wait_recv()
                own[d] = own[d] + lrecv[d].astype(F32)

            stage[d] = own[d].astype(BF)
            right_copy(d).start()

        @pl.when(has_left & (tau >= chips - 1 - z))
        def _():
            d = tau - (chips - 1 - z)
            own[d] = chip_sum(d)

            @pl.when(has_right)
            def _():
                left_copy(d).wait_recv()
                own[d] = own[d] + rrecv[d].astype(F32)

            stage[d] = own[d].astype(BF)
            left_copy(d).start()

        return carry

    early = min(2, chips)
    lax.fori_loop(0, early, term, 0)
    lax.fori_loop(0, 1, reduce_tick, 0)
    lax.fori_loop(early, chips, term, 0)

    row_tile = 256

    def norm_grad(i, carry):
        at = pl.ds(pl.multiple_of(i * row_tile, row_tile), row_tile)
        gnorm[:, at] = dot(gpre[...], wall[at, :proj], NT)
        return carry

    lax.fori_loop(0, model // row_tile, norm_grad, 0)
    grad_in = g_ref[0].astype(F32) + norm_back(gnorm[...], normed_ref[...], inverse_b)
    bwd_out[...] = grad_in.astype(BF)
    send_bwd = remote(bwd_out, prev_ref.at[0], pipe_sems.at[0], pipe_sems.at[1], behind)
    send_bwd.start()

    project(xnf, False)
    _, _, _, mixed_f = attend(jagged_mask(lf_ref, count))
    gated_f = (layer_norm(mixed_f)[0] * hidden[:, :hid].astype(F32)).astype(BF)
    result = xf_ref[0].astype(F32) + dot(gated_f, wall[:, proj:], NT)
    fwd_out[...] = result.astype(BF)
    send_fwd = remote(fwd_out, next_ref.at[0], pipe_sems.at[2], pipe_sems.at[3], ahead)
    send_fwd.start()

    lax.fori_loop(1, chips - 1, reduce_tick, 0)
    own[z] = chip_sum(z)

    @pl.when(has_left)
    def _():
        right_copy(z).wait_recv()
        own[z] = own[z] + lrecv[z].astype(F32)

    @pl.when(has_right)
    def _():
        left_copy(z).wait_recv()
        own[z] = own[z] + rrecv[z].astype(F32)

    gp_ref[0] = own[z, :, :proj]
    go_ref[...] = own[z, :, proj:]

    send_bwd.wait()
    send_fwd.wait()

    def drain(j, carry):
        to_partner(j).wait_send()
        part_copy(j).wait_send()

        @pl.when(has_right & (j <= z))
        def _():
            to_right(j).wait_send()

        @pl.when(has_left & (j >= z))
        def _():
            to_left(j).wait_send()

        @pl.when(j != z)
        def _():
            right_copy(j).wait_send()

        return carry

    lax.fori_loop(0, chips, drain, 0)


def per_device(acts_fwd, acts_bwd, cotangent, lens_fwd, lens_bwd, w_proj, w_out):
    chips = lax.axis_size("dp") // CORES
    phases = lax.axis_size("pipe")
    _, count, model = acts_fwd.shape
    _, shard, proj = w_proj.shape
    hid = w_out.shape[1]
    wide = proj + hid
    weights = jnp.concatenate([w_proj[0], w_out[0].T], axis=1).astype(BF)
    vmem = pl.BlockSpec(memory_space=pltpu.VMEM)
    smem = pl.BlockSpec(memory_space=pltpu.SMEM)
    dma = pltpu.SemaphoreType.DMA
    flops = 2 * count * model * (2 * proj + 2 * proj + 4 * hid)
    next_acts, prev_grads, grad_proj, grad_out = pl.pallas_call(
        functools.partial(kernel, chips, phases),
        out_shape=(
            jax.ShapeDtypeStruct((1, count, model), BF),
            jax.ShapeDtypeStruct((1, count, model), BF),
            jax.ShapeDtypeStruct((1, shard, proj), F32),
            jax.ShapeDtypeStruct((shard, hid), F32),
        ),
        in_specs=[vmem, vmem, vmem, smem, smem, vmem],
        out_specs=(vmem, vmem, vmem, vmem),
        scratch_shapes=[
            pltpu.VMEM((model, wide), BF),
            pltpu.VMEM((count, model), BF),
            pltpu.VMEM((count, model), BF),
            pltpu.VMEM((count, model), F32),
            pltpu.VMEM((model, count), BF),
            pltpu.VMEM((model, count), BF),
            pltpu.VMEM((count, proj), BF),
            pltpu.VMEM((count, proj), F32),
            pltpu.VMEM((count, proj), BF),
            pltpu.VMEM((count, hid), BF),
            pltpu.VMEM((count, model), F32),
            pltpu.VMEM((count, model), BF),
            pltpu.VMEM((count, model), BF),
            pltpu.VMEM((chips, shard, wide), F32),
            pltpu.VMEM((chips, shard, wide), BF),
            pltpu.VMEM((chips, shard, wide), BF),
            pltpu.VMEM((chips, shard, wide), BF),
            pltpu.VMEM((chips, shard, wide), BF),
            pltpu.VMEM((chips, shard, wide), BF),
        ]
        + [dma((chips,))] * 10
        + [dma((4,))],
        compiler_params=pltpu.CompilerParams(
            collective_id=0, has_side_effects=True, vmem_limit_bytes=56 * 1024 * 1024
        ),
        cost_estimate=pl.CostEstimate(
            flops=flops, bytes_accessed=4 * model * wide, transcendentals=2 * count * proj
        ),
    )(acts_fwd, acts_bwd, cotangent, lens_fwd, lens_bwd, weights)
    return next_acts, prev_grads, grad_proj, grad_out.T[None]


def solution(mesh):
    return jax.shard_map(
        per_device,
        mesh=mesh,
        in_specs=(
            P("pipe", "dp", None),
            P("pipe", "dp", None),
            P("pipe", "dp", None),
            P("pipe", "dp", None),
            P("pipe", "dp", None),
            P("pipe", "dp", None),
            P("pipe", None, "dp"),
        ),
        out_specs=(
            P("pipe", "dp", None),
            P("pipe", "dp", None),
            P("pipe", "dp", None),
            P("pipe", None, "dp"),
        ),
        check_vma=False,
    )
```

time: 172 us -> 93.3 us (0.54)
  waiting for transfers between devices: 107 us -> 0 us
  Pallas kernels: 0 us -> 84.3 us
  matrix products: 17.5 us -> 0 us
  blocking collectives: 17.1 us -> 0 us
  between operations: 14.1 us -> 0.66 us
  other arithmetic: 8.35 us -> 2.93 us
  starting transfers between devices: 3.16 us -> 0 us
    pallas_call x0 -> x1, Pallas kernels: none -> 84.3 us  [per_device(): pl.pallas_call(functools.partial(kernel, chips, phases), out_shape=(jax.S...]
    reduce_scatter x2 -> x0, waiting for transfers between devices: 62.6 us -> none  [the longest x1 62.6 us: per_device(): lax.psum_scatter(term_proj, 'dp', scatter_dimension=0, tiled=True)]
    all_gather x1 -> x0, waiting for transfers between devices: 38.8 us -> none  [per_device(): lax.all_gather(w_proj[0].astype(jnp.bfloat16), 'dp', axis=0, tiled=True)]
    dot_general x14 -> x0, matrix products: 17.5 us -> none  [the longest x2 5.3 us: forward_parts(): preact = jnp.dot(normed_bf, w_first, preferred_element_type=jnp.float32)]
    all_gather x1 -> x0, blocking collectives: 17.1 us -> none  [per_device(): lax.all_gather(w_out[0].astype(jnp.bfloat16), 'dp', axis=1, tiled=True)]
    ppermute x2 -> x0, waiting for transfers between devices: 6.01 us -> none  [passed_along(): lax.ppermute(array, axis, [(i, (i + by) % count) for i in range(count)])]
    convert_element_type x6 -> x0, other arithmetic: 3.64 us -> none  [the longest x1 1.92 us: per_device(): w_proj[0].astype(jnp.bfloat16)]
    ppermute x2 -> x0, starting transfers between devices: 3.04 us -> none  [passed_along(): lax.ppermute(array, axis, [(i, (i + by) % count) for i in range(count)])]
  transfers between devices with their start and end apart: 5 -> 0, of which waited for: 4 -> 0; matrix products, arithmetic and copies ran while one was open for 11% -> 0% of each run, Pallas kernels for 0% -> 0%
where the time goes in v1:
time: 93.3 us; the launch traced here: 93 us
  Pallas kernels  84.3 us (90%)
  local copies, waits for them, and re-layouts  5.1 us (5%)
  other arithmetic  2.93 us (3%)
    pallas_call x1, Pallas kernels, per_device(): pl.pallas_call(functools.partial(kernel, chips, phases), out_shape=(jax.S...  84.3 us
    unnamed x8, local copies, waits for them, and re-layouts  5.1 us

profile of v1, /device:TPU:0, one launch (start us, length us, event | category | flops | bytes accessed | tf_op | source)
XLA Modules:
  0.0 93.0 jit_solution(17622258666758731250)
XLA Ops:
  0.6 0.9 %convert_bitcast_fusion.1 = bf16[96,512]{1,0:T(8,128)(2,1)S(1)} fusion(f32[1,512,96]{1,2,0:T(8,128)} %param.13), kind=kLoop, calls=%fused_computation.2 | loop fusion | flops 49152 | bytes 294912 | tf_op jit(solution)/shard_map/transpose | solution.py:402
  1.6 1.2 %convert_bitcast_fusion = bf16[96,2048]{1,0:T(8,128)(2,1)S(1)} fusion(f32[1,96,2048]{2,1,0:T(8,128)} %param.12), kind=kLoop, calls=%fused_computation.1 | loop fusion | flops 196608 | bytes 1179648 | tf_op jit(solution)/shard_map/squeeze | solution.py:402
  2.8 0.8 pad_maximum_fusion.w_ref
  3.6 84.3 %shard_map.102 = (bf16[1,128,768]{2,1,0:T(8,128)(2,1)}, bf16[1,128,768]{2,1,0:T(8,128)(2,1)}, f32[1,96,2048]{2,1,0:T(8,128)}, f32[96,512]{1,0:T(8,128)}) custom-call(bf16[1,128,768]{2,1,0:T(8,128)(2,1)} %xf_ref.1, bf16[1,128,768]{2,1,0:T(8,128)(2,1)} %xb_ref.1, bf16[1,128,768]{2,1,0:T(8,128)(2,1)} %g_ref.1, s32[1,1,4]{2,1,0:T(1,128)} %lf_ref.1, ...), custom_call_target="tpu_custom_call" | custom-call | flops 2013265920 | bytes 7864320 | tf_op jit(solution)/shard_map/pallas_call | solution.py:407
  87.9 0.0 copy-start
  87.9 1.7 %copy.15 = bf16[1,128,768]{2,1,0:T(8,128)(2,1)} copy(bf16[1,128,768]{2,1,0:T(8,128)(2,1)} %get-tuple-element.16) | data formatting | bytes 393216
  89.6 1.6 %copy.16 = bf16[1,128,768]{2,1,0:T(8,128)(2,1)} copy(bf16[1,128,768]{2,1,0:T(8,128)(2,1)} %get-tuple-element.17) | data formatting | bytes 393216
  91.2 0.0 copy-done
  91.2 0.0 copy-start.1
  91.2 0.9 copy.17
  92.1 0.2 copy-done.1
  92.3 0.7 copy.18
Async XLA Ops:
  87.9 3.3 %copy-start = (f32[1,96,2048]{2,1,0:T(8,128)S(1)}, f32[1,96,2048]{2,1,0:T(8,128)}, u32[]{:S(2)}) copy-start(f32[1,96,2048]{2,1,0:T(8,128)} %get-tuple-element.18) | copy-start | bytes 2359300
  91.2 1.1 %copy-start.1 = (f32[96,512]{1,0:T(8,128)S(1)}, f32[96,512]{1,0:T(8,128)}, u32[]{:S(2)}) copy-start(f32[96,512]{1,0:T(8,128)} %get-tuple-element.11) | copy-start | bytes 589828

commit v2 on v1

v2 whole, which is shorter than its diff:
```python
import functools
import math

import jax
import jax.numpy as jnp
from jax import lax
from jax.experimental import pallas as pl
from jax.experimental.pallas import tpu as pltpu
from jax.sharding import PartitionSpec as P

HEADS = 4
HEAD_DIM = 128
LMAX = 64
EPS = 1e-05
CORES = 2
PARTS = 5
MESH = pl.DeviceIdType.MESH
BF = jnp.bfloat16
F32 = jnp.float32

NN = (((1,), (0,)), ((), ()))
NT = (((1,), (1,)), ((), ()))
TN = (((0,), (0,)), ((), ()))


def dot(a, b, dims=NN):
    return lax.dot_general(a, b, dims, preferred_element_type=F32)


def sigmoid(v):
    return 0.5 + 0.5 * jnp.tanh(0.5 * v)


def layer_norm(values):
    center = values - jnp.mean(values, axis=-1, keepdims=True)
    inverse = lax.rsqrt(jnp.mean(center * center, axis=-1, keepdims=True) + EPS)
    return center * inverse, inverse


def norm_back(grad, normed, inverse):
    return inverse * (
        grad
        - jnp.mean(grad, axis=-1, keepdims=True)
        - normed * jnp.mean(grad * normed, axis=-1, keepdims=True)
    )


def jagged_mask(lens_ref, count):
    rows = lax.broadcasted_iota(jnp.int32, (count, count), 0)
    cols = lax.broadcasted_iota(jnp.int32, (count, count), 1)
    row_seg = jnp.zeros((count, count), jnp.int32)
    col_seg = jnp.zeros((count, count), jnp.int32)
    end = jnp.int32(0)
    for user in range(lens_ref.shape[2]):
        end = end + lens_ref[0, 0, user]
        row_seg += jnp.where(rows >= end, 1, 0)
        col_seg += jnp.where(cols >= end, 1, 0)
    keep = (row_seg == col_seg) & (cols <= rows)
    return jnp.where(keep, 1.0 / LMAX, 0.0)


def kernel(
    chips,
    phases,
    xf_ref,
    xb_ref,
    g_ref,
    lf_ref,
    lb_ref,
    wp_ref,
    wo_ref,
    next_ref,
    prev_ref,
    gp_ref,
    go_ref,
    wall,
    xnf,
    xnb,
    normed_ref,
    norm_t,
    g_t,
    hidden,
    slope,
    gpre,
    gated_b,
    gnorm,
    fwd_out,
    bwd_out,
    own,
    psend,
    precv,
    lrecv,
    rrecv,
    stage,
    ag_right,
    ag_left,
    ag_part,
    ag_chain,
    ag_precv,
    rs_send,
    rs_part,
    rs_precv,
    rs_lrecv,
    rs_rrecv,
    pipe_sems,
):
    val, que, key, gat, out = range(PARTS)
    shard, hid = wo_ref.shape
    count, model = xf_ref.shape[1:]
    scale = HEAD_DIM ** (-0.5)
    loss_scale = 1.0 / math.sqrt(chips * CORES * count)
    me = lax.axis_index("dp")
    phase = lax.axis_index("pipe")
    z, c = lax.div(me, CORES), lax.rem(me, CORES)
    has_left, has_right = z > 0, z < chips - 1
    middle = has_left & has_right
    end = jnp.logical_not(middle)
    left, right, partner = {"dp": me - CORES}, {"dp": me + CORES}, {"dp": z * CORES + 1 - c}
    ahead = {"pipe": lax.rem(phase + 1, phases)}
    behind = {"pipe": lax.rem(phase + phases - 1, phases)}

    barrier = pltpu.get_barrier_semaphore()

    def greet(target):
        pl.semaphore_signal(barrier, inc=1, device_id=target, device_id_type=MESH)

    @pl.when(has_left)
    def _():
        greet(left)

    @pl.when(has_right)
    def _():
        greet(right)

    greet(partner)
    greet(ahead)
    greet(behind)

    def rows(chip, core):
        return pl.ds(pl.multiple_of((chip * CORES + core) * shard, shard), shard)

    def home(i):
        start = (i + 1) % (PARTS - 1) * hid
        return slice(start, start + hid)

    for i in (val, que, key, gat):
        wall[i, rows(z, c), :] = wp_ref[0, :, home(i)].astype(BF)
    wall[out, rows(z, c), :] = wo_ref[...].astype(BF)

    neighbours = 3 + jnp.where(has_left, 1, 0) + jnp.where(has_right, 1, 0)
    pl.semaphore_wait(barrier, neighbours)

    def remote(src, dst, send_sem, recv_sem, target):
        return pltpu.make_async_remote_copy(
            src_ref=src,
            dst_ref=dst,
            send_sem=send_sem,
            recv_sem=recv_sem,
            device_id=target,
            device_id_type=MESH,
        )

    def gather(i, chip, core, send_sem, recv_sem, target):
        block = wall.at[i, rows(chip, core), :]
        return remote(block, block, send_sem.at[i, chip], recv_sem.at[i, chip], target)

    def to_right(i, chip):
        return gather(i, chip, c, ag_right, ag_chain, right)

    def to_left(i, chip):
        return gather(i, chip, c, ag_left, ag_chain, left)

    def to_partner(i, chip):
        return gather(i, chip, c, ag_part, ag_precv, partner)

    def from_partner(i, chip):
        return gather(i, chip, 1 - c, ag_part, ag_precv, partner)

    def start_own(i):
        @pl.when(has_right)
        def _():
            to_right(i, z).start()

        @pl.when(has_left)
        def _():
            to_left(i, z).start()

        to_partner(i, z).start()

    def loop(lower, upper, body):
        def step(i, carry):
            body(i)
            return carry

        lax.fori_loop(lower, upper, step, 0)

    ahead_parts = 2
    loop(0, ahead_parts, start_own)

    @pl.when(end)
    def _():
        loop(ahead_parts, PARTS, start_own)

    normed_b, inverse_b = layer_norm(xb_ref[0].astype(F32))
    normed_ref[...] = normed_b
    xnb[...] = normed_b.astype(BF)
    normed_f, _ = layer_norm(xf_ref[0].astype(F32))
    xnf[...] = normed_f.astype(BF)
    norm_t[...] = normed_b.T.astype(BF)
    g_t[...] = g_ref[0].astype(F32).T.astype(BF)
    keep_b = jagged_mask(lb_ref, count)

    def relay(i):
        def tick(t):
            from_left, from_right = z - t, z + t

            @pl.when(from_left >= 0)
            def _():
                to_right(i, from_left).wait_recv()

                @pl.when(has_right)
                def _():
                    to_right(i, from_left).start()

                to_partner(i, from_left).start()

            @pl.when(from_right < chips)
            def _():
                to_left(i, from_right).wait_recv()

                @pl.when(has_left)
                def _():
                    to_left(i, from_right).start()

                to_partner(i, from_right).start()

        loop(1, chips, tick)

    def arrivals(i):
        loop(0, chips, lambda j: from_partner(i, j).wait_recv())

    def project(x_ref, i, with_slope):
        value = dot(x_ref[...], wall[i])
        sigma = sigmoid(value)
        silu = value * sigma
        hidden[i] = silu.astype(BF)
        if with_slope:
            slope[i] = sigma + silu * (1.0 - sigma)

    def part(i, head):
        return hidden[i, :, head * HEAD_DIM : (head + 1) * HEAD_DIM]

    def attend(keep):
        sigmas, scores, attns, mixed = [], [], [], []
        for head in range(HEADS):
            score = dot(part(que, head), part(key, head), NT) * scale
            sigma = sigmoid(score)
            attn = (score * sigma * keep).astype(BF)
            mixed.append(dot(attn, part(val, head)))
            scores.append(score)
            sigmas.append(sigma)
            attns.append(attn)
        return sigmas, scores, attns, jnp.concatenate(mixed, axis=1)

    def send_forward():
        return remote(fwd_out, next_ref.at[0], pipe_sems.at[2], pipe_sems.at[3], ahead)

    def send_backward():
        return remote(bwd_out, prev_ref.at[0], pipe_sems.at[0], pipe_sems.at[1], behind)

    def forward_block():
        loop(0, PARTS - 1, lambda i: project(xnf, i, False))
        _, _, _, mixed_f = attend(jagged_mask(lf_ref, count))
        gated_f = (layer_norm(mixed_f)[0] * hidden[gat].astype(F32)).astype(BF)
        result = xf_ref[0].astype(F32) + dot(gated_f, wall[out], NT)
        fwd_out[...] = result.astype(BF)
        send_forward().start()

    def part_copy(i, d):
        return remote(psend.at[i, d], precv.at[i, d], rs_part.at[i, d], rs_precv.at[i, d], partner)

    def right_copy(i, d):
        return remote(stage.at[i, d], lrecv.at[i, d], rs_send.at[i, d], rs_lrecv.at[i, d], right)

    def left_copy(i, d):
        return remote(stage.at[i, d], rrecv.at[i, d], rs_send.at[i, d], rs_rrecv.at[i, d], left)

    def terms(i):
        sides, factor = (g_t, gated_b[...]) if i == out else (norm_t, gpre[i])

        def term(k):
            d = jnp.where(z < chips // 2, chips - 1 - k, k)
            psend[i, d] = (dot(sides[rows(d, 1 - c), :], factor) * loss_scale).astype(BF)
            part_copy(i, d).start()
            own[i, d] = dot(sides[rows(d, c), :], factor) * loss_scale

        loop(0, chips, term)

    def chip_sum(i, d):
        part_copy(i, d).wait_recv()
        return own[i, d] + precv[i, d].astype(F32)

    def reduce(i):
        def tick(tau):
            @pl.when(has_right & (tau >= z))
            def _():
                d = chips - 1 - tau + z
                own[i, d] = chip_sum(i, d)

                @pl.when(has_left)
                def _():
                    right_copy(i, d).wait_recv()
                    own[i, d] = own[i, d] + lrecv[i, d].astype(F32)

                stage[i, d] = own[i, d].astype(BF)
                right_copy(i, d).start()

            @pl.when(has_left & (tau >= chips - 1 - z))
            def _():
                d = tau - (chips - 1 - z)
                own[i, d] = chip_sum(i, d)

                @pl.when(has_right)
                def _():
                    left_copy(i, d).wait_recv()
                    own[i, d] = own[i, d] + rrecv[i, d].astype(F32)

                stage[i, d] = own[i, d].astype(BF)
                left_copy(i, d).start()

        loop(0, chips - 1, tick)

    @pl.when(middle)
    def _():
        def pass_on(i):
            relay(i)

            @pl.when(i + ahead_parts < PARTS)
            def _():
                start_own(i + ahead_parts)

        loop(0, PARTS, pass_on)
        loop(0, PARTS, arrivals)
        forward_block()

    @pl.when(end)
    def _():
        loop(0, gat, relay)
        loop(0, gat, arrivals)

    loop(0, gat, lambda i: project(xnb, i, True))
    sigmas, scores, attns, mixed = attend(keep_b)
    mixed_n, inverse_o = layer_norm(mixed)

    @pl.when(end)
    def _():
        relay(gat)
        arrivals(gat)

    project(xnb, gat, True)
    gate = hidden[gat].astype(F32)
    gated_b[...] = (mixed_n * gate).astype(BF)
    terms(out)

    @pl.when(end)
    def _():
        reduce(out)
        relay(out)
        arrivals(out)

    grad_y = dot(g_ref[0], wall[out])
    gpre[gat] = (grad_y * mixed_n * slope[gat]).astype(BF)
    terms(gat)
    grad_mixed = norm_back(grad_y * gate, mixed_n, inverse_o).astype(BF)
    heads = [slice(head * HEAD_DIM, (head + 1) * HEAD_DIM) for head in range(HEADS)]
    for head, cols in enumerate(heads):
        grad_vals = dot(attns[head], grad_mixed[:, cols], TN)
        gpre[val, :, cols] = (grad_vals * slope[val, :, cols]).astype(BF)
    terms(val)

    @pl.when(end)
    def _():
        reduce(gat)

    for head, cols in enumerate(heads):
        score, sigma = scores[head], sigmas[head]
        grad_attn = dot(grad_mixed[:, cols], part(val, head), NT)
        grad_s = (
            grad_attn * keep_b * (sigma * (1.0 + score * (1.0 - sigma))) * scale
        ).astype(BF)
        grad_q = dot(grad_s, part(key, head))
        grad_k = dot(grad_s, part(que, head), TN)
        gpre[que, :, cols] = (grad_q * slope[que, :, cols]).astype(BF)
        gpre[key, :, cols] = (grad_k * slope[key, :, cols]).astype(BF)
    terms(que)

    @pl.when(end)
    def _():
        reduce(val)

    terms(key)

    @pl.when(end)
    def _():
        reduce(que)
        reduce(key)

    @pl.when(middle)
    def _():
        reduce(out)
        reduce(gat)

    row_tile = 256

    def norm_grad(n):
        at = pl.ds(pl.multiple_of(n * row_tile, row_tile), row_tile)
        total = dot(gpre[val], wall[val, at, :], NT)
        for i in (que, key, gat):
            total += dot(gpre[i], wall[i, at, :], NT)
        gnorm[:, at] = total

    loop(0, model // row_tile, norm_grad)
    grad_in = g_ref[0].astype(F32) + norm_back(gnorm[...], normed_ref[...], inverse_b)
    bwd_out[...] = grad_in.astype(BF)
    send_backward().start()

    @pl.when(middle)
    def _():
        reduce(val)
        reduce(que)
        reduce(key)

    @pl.when(end)
    def _():
        forward_block()

    for i in (out, gat, val, que, key):
        own[i, z] = chip_sum(i, z)

        @pl.when(has_left)
        def _():
            right_copy(i, z).wait_recv()
            own[i, z] = own[i, z] + lrecv[i, z].astype(F32)

        @pl.when(has_right)
        def _():
            left_copy(i, z).wait_recv()
            own[i, z] = own[i, z] + rrecv[i, z].astype(F32)

        if i == out:
            go_ref[...] = own[i, z]
        else:
            gp_ref[0, :, home(i)] = own[i, z]

    send_backward().wait()
    send_forward().wait()

    def drain(j):
        def each(i):
            to_partner(i, j).wait_send()
            part_copy(i, j).wait_send()

            @pl.when(has_right & (j <= z))
            def _():
                to_right(i, j).wait_send()

            @pl.when(has_left & (j >= z))
            def _():
                to_left(i, j).wait_send()

            @pl.when(j != z)
            def _():
                right_copy(i, j).wait_send()

        loop(0, PARTS, each)

    loop(0, chips, drain)


def finish(*refs):
    sems = refs[-1]
    half = (len(refs) - 1) // 2
    copies = [
        pltpu.make_async_copy(src, dst, sems.at[n])
        for n, (src, dst) in enumerate(zip(refs[:half], refs[half:-1]))
    ]
    for copy in copies:
        copy.start()
    for copy in copies:
        copy.wait()


def per_device(acts_fwd, acts_bwd, cotangent, lens_fwd, lens_bwd, w_proj, w_out):
    chips = lax.axis_size("dp") // CORES
    phases = lax.axis_size("pipe")
    _, count, model = acts_fwd.shape
    _, shard, proj = w_proj.shape
    hid = w_out.shape[1]
    vmem = pl.BlockSpec(memory_space=pltpu.VMEM)
    smem = pl.BlockSpec(memory_space=pltpu.SMEM)
    hbm = pl.BlockSpec(memory_space=pl.ANY)
    dma = pltpu.SemaphoreType.DMA
    slots = pltpu.VMEM((PARTS, chips, shard, hid), BF)
    flops = 2 * count * model * (2 * proj + 2 * proj + 4 * hid)
    results = (
        jax.ShapeDtypeStruct((1, count, model), BF),
        jax.ShapeDtypeStruct((1, count, model), BF),
        jax.ShapeDtypeStruct((1, shard, proj), F32),
        jax.ShapeDtypeStruct((shard, hid), F32),
    )
    outs = pl.pallas_call(
        functools.partial(kernel, chips, phases),
        out_shape=results,
        in_specs=[vmem, vmem, vmem, smem, smem, vmem, vmem],
        out_specs=(vmem, vmem, vmem, vmem),
        scratch_shapes=[
            pltpu.VMEM((PARTS, model, hid), BF),
            pltpu.VMEM((count, model), BF),
            pltpu.VMEM((count, model), BF),
            pltpu.VMEM((count, model), F32),
            pltpu.VMEM((model, count), BF),
            pltpu.VMEM((model, count), BF),
            pltpu.VMEM((PARTS - 1, count, hid), BF),
            pltpu.VMEM((PARTS - 1, count, hid), F32),
            pltpu.VMEM((PARTS - 1, count, hid), BF),
            pltpu.VMEM((count, hid), BF),
            pltpu.VMEM((count, model), F32),
            pltpu.VMEM((count, model), BF),
            pltpu.VMEM((count, model), BF),
            pltpu.VMEM((PARTS, chips, shard, hid), F32),
            slots,
            slots,
            slots,
            slots,
            slots,
        ]
        + [dma((PARTS, chips))] * 10
        + [dma((4,))],
        compiler_params=pltpu.CompilerParams(
            collective_id=0, has_side_effects=True, vmem_limit_bytes=56 * 1024 * 1024
        ),
        cost_estimate=pl.CostEstimate(
            flops=flops,
            bytes_accessed=4 * shard * (proj + hid),
            transcendentals=2 * count * proj,
        ),
    )(acts_fwd, acts_bwd, cotangent, lens_fwd, lens_bwd, w_proj, w_out[0].T)
    next_acts, prev_grads, grad_proj, grad_out = pl.pallas_call(
        finish,
        out_shape=results,
        in_specs=[hbm] * 4,
        out_specs=(hbm,) * 4,
        scratch_shapes=[dma((4,))],
    )(*outs)
    return next_acts, prev_grads, grad_proj, grad_out.T[None]


def solution(mesh):
    return jax.shard_map(
        per_device,
        mesh=mesh,
        in_specs=(
            P("pipe", "dp", None),
            P("pipe", "dp", None),
            P("pipe", "dp", None),
            P("pipe", "dp", None),
            P("pipe", "dp", None),
            P("pipe", "dp", None),
            P("pipe", None, "dp"),
        ),
        out_specs=(
            P("pipe", "dp", None),
            P("pipe", "dp", None),
            P("pipe", "dp", None),
            P("pipe", None, "dp"),
        ),
        check_vma=False,
    )
```

time: 93.3 us -> 125 us (1.34)
  Pallas kernels: 84.3 us -> 124 us
  local copies, waits for them, and re-layouts: 5.1 us -> 0 us
  other arithmetic: 2.93 us -> 0 us
    pallas_call x1 -> x2, Pallas kernels: 84.3 us -> 124 us  [the longest x1 81.5 us: per_device(): pl.pallas_call(functools.partial(kernel, chips, phases), out_shape=result...]
    unnamed x8 -> x0, local copies, waits for them, and re-layouts: 5.1 us -> none
where the time goes in v2:
time: 125 us
  Pallas kernels  124 us (99%)
    pallas_call x1, Pallas kernels, per_device(): pl.pallas_call(functools.partial(kernel, chips, phases), out_shape=result...  81.5 us
    pallas_call x1, Pallas kernels, per_device(): pl.pallas_call(finish, out_shape=results, in_specs=[hbm] * 4, out_specs=(...  42.8 us

profile of v2, /device:TPU:0, one launch (start us, length us, event | category | flops | bytes accessed | tf_op | source)
XLA Modules:
  0.0 125.0 jit_solution(7153912224545490724)
XLA Ops:
  0.6 81.5 %shard_map.102 = (bf16[1,128,768]{2,1,0:T(8,128)(2,1)}, bf16[1,128,768]{2,1,0:T(8,128)(2,1)}, f32[1,96,2048]{2,1,0:T(8,128)}, f32[96,512]{1,0:T(8,128)}) custom-call(bf16[1,128,768]{2,1,0:T(8,128)(2,1)} %xf_ref.1, bf16[1,128,768]{2,1,0:T(8,128)(2,1)} %xb_ref.1, bf16[1,128,768]{2,1,0:T(8,128)(2,1)} %g_ref.1, s32[1,1,4]{2,1,0:T(1,128)} %lf_ref.1, ...), custom_call_target="tpu_custom_call" | custom-call | flops 2013265920 | bytes 983040 | tf_op jit(solution)/shard_map/pallas_call | solution.py:511
  82.2 42.8 %shard_map.103 = (bf16[1,128,768]{2,1,0:T(8,128)(2,1)}, bf16[1,128,768]{2,1,0:T(8,128)(2,1)}, f32[1,96,2048]{2,1,0:T(8,128)}, f32[96,512]{1,0:T(8,128)}) custom-call(bf16[1,128,768]{2,1,0:T(8,128)(2,1)} %get-tuple-element.12.refs_0_, bf16[1,128,768]{2,1,0:T(8,128)(2,1)} %get-tuple-element.13.refs_1_, f32[1,96,2048]{2,1,0:T(8,128)} %get-tuple-element.14.refs_2_, ...), custom_call_target="tpu_custom_call" | custom-call | tf_op jit(solution)/shard_map/pallas_call | solution.py:548

commit v3 on v2

--- a/solution.py
+++ b/solution.py
@@ -478,16 +478,9 @@
 
 
 def finish(*refs):
-    sems = refs[-1]
-    half = (len(refs) - 1) // 2
-    copies = [
-        pltpu.make_async_copy(src, dst, sems.at[n])
-        for n, (src, dst) in enumerate(zip(refs[:half], refs[half:-1]))
-    ]
-    for copy in copies:
-        copy.start()
-    for copy in copies:
-        copy.wait()
+    half = len(refs) // 2
+    for src, dst in zip(refs[:half], refs[half:]):
+        dst[...] = src[...]
 
 
 def per_device(acts_fwd, acts_bwd, cotangent, lens_fwd, lens_bwd, w_proj, w_out):
@@ -498,7 +491,6 @@
     hid = w_out.shape[1]
     vmem = pl.BlockSpec(memory_space=pltpu.VMEM)
     smem = pl.BlockSpec(memory_space=pltpu.SMEM)
-    hbm = pl.BlockSpec(memory_space=pl.ANY)
     dma = pltpu.SemaphoreType.DMA
     slots = pltpu.VMEM((PARTS, chips, shard, hid), BF)
     flops = 2 * count * model * (2 * proj + 2 * proj + 4 * hid)
@@ -548,9 +540,8 @@
     next_acts, prev_grads, grad_proj, grad_out = pl.pallas_call(
         finish,
         out_shape=results,
-        in_specs=[hbm] * 4,
-        out_specs=(hbm,) * 4,
-        scratch_shapes=[dma((4,))],
+        in_specs=[vmem] * 4,
+        out_specs=(vmem,) * 4,
     )(*outs)
     return next_acts, prev_grads, grad_proj, grad_out.T[None]
 

time: 125 us -> 84.8 us (0.68)
  Pallas kernels: 124 us -> 84 us
    pallas_call x1, Pallas kernels: 42.8 us -> 2.44 us  [per_device(): pl.pallas_call(finish, out_shape=results, in_specs=[vmem] * 4, out_specs=...]
where the time goes in v3:
time: 84.8 us; the launch traced here: 84.6 us
  Pallas kernels  84 us (99%)
    pallas_call x1, Pallas kernels, per_device(): pl.pallas_call(functools.partial(kernel, chips, phases), out_shape=result...  81.5 us
    pallas_call x1, Pallas kernels, per_device(): pl.pallas_call(finish, out_shape=results, in_specs=[vmem] * 4, out_specs=...  2.44 us

profile of v3, /device:TPU:0, one launch (start us, length us, event | category | flops | bytes accessed | tf_op | source)
XLA Modules:
  0.0 84.6 jit_solution(8304736036840438149)
XLA Ops:
  0.6 81.5 %shard_map.102 = (bf16[1,128,768]{2,1,0:T(8,128)(2,1)}, bf16[1,128,768]{2,1,0:T(8,128)(2,1)}, f32[1,96,2048]{2,1,0:T(8,128)}, f32[96,512]{1,0:T(8,128)}) custom-call(bf16[1,128,768]{2,1,0:T(8,128)(2,1)} %xf_ref.1, bf16[1,128,768]{2,1,0:T(8,128)(2,1)} %xb_ref.1, bf16[1,128,768]{2,1,0:T(8,128)(2,1)} %g_ref.1, s32[1,1,4]{2,1,0:T(1,128)} %lf_ref.1, ...), custom_call_target="tpu_custom_call" | custom-call | flops 2013265920 | bytes 983040 | tf_op jit(solution)/shard_map/pallas_call | solution.py:503
  82.2 2.4 %shard_map.103 = (bf16[1,128,768]{2,1,0:T(8,128)(2,1)}, bf16[1,128,768]{2,1,0:T(8,128)(2,1)}, f32[1,96,2048]{2,1,0:T(8,128)}, f32[96,512]{1,0:T(8,128)}) custom-call(bf16[1,128,768]{2,1,0:T(8,128)(2,1)} %get-tuple-element.12.refs_0_, bf16[1,128,768]{2,1,0:T(8,128)(2,1)} %get-tuple-element.13.refs_1_, f32[1,96,2048]{2,1,0:T(8,128)} %get-tuple-element.14.refs_2_, ...), custom_call_target="tpu_custom_call" | custom-call | tf_op jit(solution)/shard_map/pallas_call | solution.py:540

commit v4 on v3

v4 whole, which is shorter than its diff:
```python
import functools
import math

import jax
import jax.numpy as jnp
from jax import lax
from jax.experimental import pallas as pl
from jax.experimental.pallas import tpu as pltpu
from jax.sharding import PartitionSpec as P

HEADS = 4
HEAD_DIM = 128
LMAX = 64
EPS = 1e-05
CORES = 2
PARTS = 5
MESH = pl.DeviceIdType.MESH
BF = jnp.bfloat16
F32 = jnp.float32

NN = (((1,), (0,)), ((), ()))
NT = (((1,), (1,)), ((), ()))
TN = (((0,), (0,)), ((), ()))


def dot(a, b, dims=NN):
    return lax.dot_general(a, b, dims, preferred_element_type=F32)


def sigmoid(v):
    return 0.5 + 0.5 * jnp.tanh(0.5 * v)


def layer_norm(values):
    center = values - jnp.mean(values, axis=-1, keepdims=True)
    inverse = lax.rsqrt(jnp.mean(center * center, axis=-1, keepdims=True) + EPS)
    return center * inverse, inverse


def norm_back(grad, normed, inverse):
    return inverse * (
        grad
        - jnp.mean(grad, axis=-1, keepdims=True)
        - normed * jnp.mean(grad * normed, axis=-1, keepdims=True)
    )


def jagged_mask(lens_ref, count):
    rows = lax.broadcasted_iota(jnp.int32, (count, count), 0)
    cols = lax.broadcasted_iota(jnp.int32, (count, count), 1)
    row_seg = jnp.zeros((count, count), jnp.int32)
    col_seg = jnp.zeros((count, count), jnp.int32)
    end = jnp.int32(0)
    for user in range(lens_ref.shape[2]):
        end = end + lens_ref[0, 0, user]
        row_seg += jnp.where(rows >= end, 1, 0)
        col_seg += jnp.where(cols >= end, 1, 0)
    keep = (row_seg == col_seg) & (cols <= rows)
    return jnp.where(keep, 1.0 / LMAX, 0.0)


def kernel(
    chips,
    phases,
    xf_ref,
    xb_ref,
    g_ref,
    lf_ref,
    lb_ref,
    wp_ref,
    wo_ref,
    next_ref,
    prev_ref,
    gp_ref,
    go_ref,
    wall,
    xnf,
    xnb,
    normed_ref,
    norm_t,
    g_both,
    g_t,
    hidden,
    slope,
    gpre,
    gated_b,
    gnorm,
    fwd_out,
    bwd_out,
    own,
    psend,
    precv,
    lrecv,
    rrecv,
    stage,
    final,
    masks,
    mate_acts,
    mate_masks,
    ag_right,
    ag_left,
    ag_part,
    ag_chain,
    ag_precv,
    rs_send,
    rs_part,
    rs_precv,
    rs_lrecv,
    rs_rrecv,
    fin_send,
    fin_recv,
    act_send,
    act_recv,
    pipe_send,
    pipe_recv,
):
    val, que, key, gat, out = range(PARTS)
    shard, hid = wo_ref.shape
    count, model = xf_ref.shape[1:]
    scale = HEAD_DIM ** (-0.5)
    loss_scale = 1.0 / math.sqrt(chips * CORES * count)
    me = lax.axis_index("dp")
    phase = lax.axis_index("pipe")
    z, c = lax.div(me, CORES), lax.rem(me, CORES)

    pairs = chips // 2
    m = lax.div(z, 2)

    def inner(pair):
        return 2 * pair + jnp.where(2 * pair < pairs, 1, 0)

    worker = z == inner(m)
    helper = jnp.logical_not(worker)
    other = 4 * m + 1 - z
    has_left, has_right = m > 0, m < pairs - 1
    mate_dp = other * CORES + c
    mate, partner = {"dp": mate_dp}, {"dp": z * CORES + 1 - c}
    left, right = {"dp": inner(m - 1) * CORES + c}, {"dp": inner(m + 1) * CORES + c}
    ahead = lax.rem(phase + 1, phases)
    behind = lax.rem(phase + phases - 1, phases)

    barrier = pltpu.get_barrier_semaphore()

    def greet(target):
        pl.semaphore_signal(barrier, inc=1, device_id=target, device_id_type=MESH)

    greet(mate)

    @pl.when(helper)
    def _():
        greet({"dp": mate_dp, "pipe": ahead})
        greet({"dp": mate_dp, "pipe": behind})

    @pl.when(worker)
    def _():
        greet(partner)
        greet({"pipe": ahead})
        greet({"pipe": behind})

        @pl.when(has_left)
        def _():
            greet(left)

        @pl.when(has_right)
        def _():
            greet(right)

    def rows(chip, core):
        return pl.ds(pl.multiple_of((chip * CORES + core) * shard, shard), shard)

    def home(i):
        start = (i + 1) % (PARTS - 1) * hid
        return slice(start, start + hid)

    for i in (val, que, key, gat):
        wall[i, rows(z, c), :] = wp_ref[0, :, home(i)].astype(BF)
    wall[out, rows(z, c), :] = wo_ref[...].astype(BF)

    peers = jnp.where(worker, 6 + jnp.where(has_left, 1, 0) + jnp.where(has_right, 1, 0), 1)
    pl.semaphore_wait(barrier, peers)

    def remote(src, dst, send_sem, recv_sem, target):
        return pltpu.make_async_remote_copy(
            src_ref=src,
            dst_ref=dst,
            send_sem=send_sem,
            recv_sem=recv_sem,
            device_id=target,
            device_id_type=MESH,
        )

    def gather(i, chip, core, send_sem, recv_sem, target):
        block = wall.at[i, rows(chip, core), :]
        return remote(block, block, send_sem.at[i, chip], recv_sem.at[i, chip], target)

    def to_right(i, chip):
        return gather(i, chip, c, ag_right, ag_chain, right)

    def to_left(i, chip):
        return gather(i, chip, c, ag_left, ag_chain, left)

    def to_mate(i):
        return gather(i, z, c, ag_right, ag_chain, mate)

    def to_partner(i, chip):
        return gather(i, chip, c, ag_part, ag_precv, partner)

    def from_partner(i, chip):
        return gather(i, chip, 1 - c, ag_part, ag_precv, partner)

    def act_copy(n):
        src, dst = (
            (xb_ref.at[0], mate_acts.at[0]),
            (masks, mate_masks),
            (g_ref.at[0], mate_acts.at[1]),
            (xf_ref.at[0], mate_acts.at[2]),
        )[n]
        return remote(src, dst, act_send.at[n], act_recv.at[n], mate)

    def final_copy(i):
        return remote(stage.at[i, other], final.at[i], fin_send.at[i], fin_recv.at[i], mate)

    def out_copy(n, to_mate_block):
        source, target_ref, to = ((fwd_out, next_ref, ahead), (bwd_out, prev_ref, behind))[n]
        src = source.at[pl.ds(count, count) if to_mate_block else pl.ds(0, count)]
        send = pipe_send.at[2 * n + (1 if to_mate_block else 0)]
        target = {"dp": mate_dp, "pipe": to} if to_mate_block else {"pipe": to}
        return remote(src, target_ref.at[0], send, pipe_recv.at[n], target)

    def loop(lower, upper, body):
        def step(i, carry):
            body(i)
            return carry

        lax.fori_loop(lower, upper, step, 0)

    @pl.when(helper)
    def _():
        to_mate(0).start()
        to_mate(1).start()
        act_copy(0).start()
        masks[0] = jagged_mask(lb_ref, count).astype(BF)
        masks[1] = jagged_mask(lf_ref, count).astype(BF)
        act_copy(1).start()
        for i in range(2, PARTS):
            to_mate(i).start()
        act_copy(2).start()
        act_copy(3).start()

        for i in (out, gat, val, que, key):
            final_copy(i).wait_recv()
            if i == out:
                go_ref[...] = final[i].astype(F32)
            else:
                gp_ref[0, :, home(i)] = final[i].astype(F32)
        for n in range(4):
            act_copy(n).wait_send()
        for i in range(PARTS):
            to_mate(i).wait_send()

    @pl.when(worker)
    def _():
        def send_on(i, chip):
            @pl.when(has_right)
            def _():
                to_right(i, chip).start()

            @pl.when(has_left)
            def _():
                to_left(i, chip).start()

            to_partner(i, chip).start()

        early = 2
        loop(0, early, lambda i: send_on(i, z))

        first, second = slice(0, count), slice(count, 2 * count)

        def prepare(at, tokens):
            normed, inverse = layer_norm(tokens.astype(F32))
            normed_ref[at, :] = normed
            xnb[at, :] = normed.astype(BF)
            norm_t[:, at] = normed.T.astype(BF)
            return inverse

        inverse_own = prepare(first, xb_ref[0])

        def mate_part(i):
            to_left(i, other).wait_recv()
            send_on(i, other)

            @pl.when(i + early < PARTS)
            def _():
                send_on(i + early, z)

        def line(i):
            def tick(t):
                lower, upper = m - t, m + t

                @pl.when(lower >= 0)
                def _():
                    for chip in (2 * lower, 2 * lower + 1):
                        to_right(i, chip).wait_recv()

                        @pl.when(has_right)
                        def _():
                            to_right(i, chip).start()

                        to_partner(i, chip).start()

                @pl.when(upper < pairs)
                def _():
                    for chip in (2 * upper, 2 * upper + 1):
                        to_left(i, chip).wait_recv()

                        @pl.when(has_left)
                        def _():
                            to_left(i, chip).start()

                        to_partner(i, chip).start()

            loop(1, pairs, tick)

        def arrivals(i):
            loop(0, chips, lambda j: from_partner(i, j).wait_recv())

        loop(0, PARTS, mate_part)

        act_copy(0).wait_recv()
        inverse_mate = prepare(second, mate_acts[0])
        inverse_b = jnp.concatenate([inverse_own, inverse_mate], axis=0)
        g_both[first, :] = g_ref[0]
        g_t[:, first] = g_ref[0].astype(F32).T.astype(BF)
        xnf[first, :] = layer_norm(xf_ref[0].astype(F32))[0].astype(BF)
        act_copy(1).wait_recv()
        keeps_b = [jagged_mask(lb_ref, count), mate_masks[0].astype(F32)]

        def project(x_ref, i, with_slope):
            value = dot(x_ref[...], wall[i])
            sigma = sigmoid(value)
            silu = value * sigma
            hidden[i] = silu.astype(BF)
            if with_slope:
                slope[i] = sigma + silu * (1.0 - sigma)

        heads = [slice(head * HEAD_DIM, (head + 1) * HEAD_DIM) for head in range(HEADS)]

        def attend(keeps):
            sigmas, scores, attns, blocks = [], [], [], []
            for at, keep in zip((first, second), keeps):
                mixed = []
                for cols in heads:
                    score = dot(hidden[que, at, cols], hidden[key, at, cols], NT) * scale
                    sigma = sigmoid(score)
                    attn = (score * sigma * keep).astype(BF)
                    mixed.append(dot(attn, hidden[val, at, cols]))
                    scores.append(score)
                    sigmas.append(sigma)
                    attns.append(attn)
                blocks.append(jnp.concatenate(mixed, axis=1))
            return sigmas, scores, attns, jnp.concatenate(blocks, axis=0)

        def both(pair):
            return pl.ds(2 * pair, 2)

        def part_copy(i, j):
            return remote(
                psend.at[i, both(j)], precv.at[i, both(j)], rs_part.at[i, j], rs_precv.at[i, j], partner
            )

        def right_copy(i, j):
            return remote(
                stage.at[i, both(j)], lrecv.at[i, both(j)], rs_send.at[i, j], rs_lrecv.at[i, j], right
            )

        def left_copy(i, j):
            return remote(
                stage.at[i, both(j)], rrecv.at[i, both(j)], rs_send.at[i, j], rs_rrecv.at[i, j], left
            )

        def terms(i):
            sides, factor = (g_t, gated_b[...]) if i == out else (norm_t, gpre[i])

            def term(k):
                j = jnp.where(2 * m < pairs, pairs - 1 - k, k)
                for d in (2 * j, 2 * j + 1):
                    theirs = dot(sides[rows(d, 1 - c), :], factor) * loss_scale
                    psend[i, d] = theirs.astype(BF)
                part_copy(i, j).start()
                for d in (2 * j, 2 * j + 1):
                    own[i, d] = dot(sides[rows(d, c), :], factor) * loss_scale

            loop(0, pairs, term)

        def chip_sum(i, j):
            part_copy(i, j).wait_recv()
            at = both(j)
            own[i, at] = own[i, at] + precv[i, at].astype(F32)

        def add_left(i, j):
            right_copy(i, j).wait_recv()
            own[i, both(j)] = own[i, both(j)] + lrecv[i, both(j)].astype(F32)

        def add_right(i, j):
            left_copy(i, j).wait_recv()
            own[i, both(j)] = own[i, both(j)] + rrecv[i, both(j)].astype(F32)

        def reduce(i):
            def tick(tau):
                @pl.when(has_right & (tau >= m))
                def _():
                    j = pairs - 1 - tau + m
                    chip_sum(i, j)

                    @pl.when(has_left)
                    def _():
                        add_left(i, j)

                    stage[i, both(j)] = own[i, both(j)].astype(BF)
                    right_copy(i, j).start()

                @pl.when(has_left & (tau >= pairs - 1 - m))
                def _():
                    j = tau - (pairs - 1 - m)
                    chip_sum(i, j)

                    @pl.when(has_right)
                    def _():
                        add_right(i, j)

                    stage[i, both(j)] = own[i, both(j)].astype(BF)
                    left_copy(i, j).start()

            loop(0, pairs - 1, tick)

        def conclude(i):
            chip_sum(i, m)

            @pl.when(has_left)
            def _():
                add_left(i, m)

            @pl.when(has_right)
            def _():
                add_right(i, m)

            stage[i, other] = own[i, other].astype(BF)
            final_copy(i).start()
            if i == out:
                go_ref[...] = own[i, z]
            else:
                gp_ref[0, :, home(i)] = own[i, z]

        loop(0, gat, line)
        loop(0, gat, arrivals)
        loop(0, gat, lambda i: project(xnb, i, True))
        line(gat)
        sigmas, scores, attns, mixed = attend(keeps_b)
        mixed_n, inverse_o = layer_norm(mixed)
        arrivals(gat)
        project(xnb, gat, True)
        gate = hidden[gat].astype(F32)
        gated_b[...] = (mixed_n * gate).astype(BF)
        act_copy(2).wait_recv()
        g_both[second, :] = mate_acts[1]
        g_t[:, second] = mate_acts[1].astype(F32).T.astype(BF)
        terms(out)
        line(out)
        reduce(out)
        arrivals(out)

        grad_y = dot(g_both[...], wall[out])
        gpre[gat] = (grad_y * mixed_n * slope[gat]).astype(BF)
        terms(gat)
        grad_mixed = norm_back(grad_y * gate, mixed_n, inverse_o).astype(BF)
        reduce(gat)
        blocks = [(b, at, n, cols) for b, at in enumerate((first, second)) for n, cols in enumerate(heads)]
        for b, at, n, cols in blocks:
            grad_vals = dot(attns[b * HEADS + n], grad_mixed[at, cols], TN)
            gpre[val, at, cols] = (grad_vals * slope[val, at, cols]).astype(BF)
        terms(val)
        for b, at, n, cols in blocks:
            score, sigma = scores[b * HEADS + n], sigmas[b * HEADS + n]
            grad_attn = dot(grad_mixed[at, cols], hidden[val, at, cols], NT)
            grad_s = (
                grad_attn * keeps_b[b] * (sigma * (1.0 + score * (1.0 - sigma))) * scale
            ).astype(BF)
            grad_q = dot(grad_s, hidden[key, at, cols])
            grad_k = dot(grad_s, hidden[que, at, cols], TN)
            gpre[que, at, cols] = (grad_q * slope[que, at, cols]).astype(BF)
            gpre[key, at, cols] = (grad_k * slope[key, at, cols]).astype(BF)
        reduce(val)
        terms(que)
        terms(key)
        reduce(que)
        reduce(key)

        row_tile = 256

        def norm_grad(n):
            at = pl.ds(pl.multiple_of(n * row_tile, row_tile), row_tile)
            total = dot(gpre[val], wall[val, at, :], NT)
            for i in (que, key, gat):
                total += dot(gpre[i], wall[i, at, :], NT)
            gnorm[:, at] = total

        loop(0, model // row_tile, norm_grad)
        grad_in = g_both[...].astype(F32) + norm_back(gnorm[...], normed_ref[...], inverse_b)
        bwd_out[...] = grad_in.astype(BF)
        out_copy(1, True).start()
        out_copy(1, False).start()
        conclude(out)

        act_copy(3).wait_recv()
        xnf[second, :] = layer_norm(mate_acts[2].astype(F32))[0].astype(BF)
        loop(0, PARTS - 1, lambda i: project(xnf, i, False))
        conclude(gat)
        keeps_f = [jagged_mask(lf_ref, count), mate_masks[1].astype(F32)]
        mixed_f = attend(keeps_f)[3]
        gated_f = (layer_norm(mixed_f)[0] * hidden[gat].astype(F32)).astype(BF)
        conclude(val)
        change = dot(gated_f, wall[out], NT)
        fwd_out[second, :] = (mate_acts[2].astype(F32) + change[second]).astype(BF)
        out_copy(0, True).start()
        fwd_out[first, :] = (xf_ref[0].astype(F32) + change[first]).astype(BF)
        out_copy(0, False).start()
        conclude(que)
        conclude(key)

        for n in range(2):
            out_copy(n, True).wait_send()
            out_copy(n, False).wait_send()

        def drain(i):
            final_copy(i).wait_send()

            def each(j):
                to_partner(i, j).wait_send()

                @pl.when(has_right & (lax.div(j, 2) <= m))
                def _():
                    to_right(i, j).wait_send()

                @pl.when(has_left & (lax.div(j, 2) >= m))
                def _():
                    to_left(i, j).wait_send()

            loop(0, chips, each)

            def pair_sends(j):
                part_copy(i, j).wait_send()

                @pl.when(j != m)
                def _():
                    right_copy(i, j).wait_send()

            loop(0, pairs, pair_sends)

        loop(0, PARTS, drain)

    for n in range(2):
        out_copy(n, False).wait_recv()


def finish(*refs):
    half = len(refs) // 2
    for src, dst in zip(refs[:half], refs[half:]):
        dst[...] = src[...]


def per_device(acts_fwd, acts_bwd, cotangent, lens_fwd, lens_bwd, w_proj, w_out):
    chips = lax.axis_size("dp") // CORES
    phases = lax.axis_size("pipe")
    _, count, model = acts_fwd.shape
    _, shard, proj = w_proj.shape
    hid = w_out.shape[1]
    vmem = pl.BlockSpec(memory_space=pltpu.VMEM)
    smem = pl.BlockSpec(memory_space=pltpu.SMEM)
    dma = pltpu.SemaphoreType.DMA
    slots = pltpu.VMEM((PARTS, chips, shard, hid), BF)
    flops = 2 * count * model * (2 * proj + 2 * proj + 4 * hid)
    results = (
        jax.ShapeDtypeStruct((1, count, model), BF),
        jax.ShapeDtypeStruct((1, count, model), BF),
        jax.ShapeDtypeStruct((1, shard, proj), F32),
        jax.ShapeDtypeStruct((shard, hid), F32),
    )
    outs = pl.pallas_call(
        functools.partial(kernel, chips, phases),
        out_shape=results,
        in_specs=[vmem, vmem, vmem, smem, smem, vmem, vmem],
        out_specs=(vmem, vmem, vmem, vmem),
        scratch_shapes=[
            pltpu.VMEM((PARTS, model, hid), BF),
            pltpu.VMEM((2 * count, model), BF),
            pltpu.VMEM((2 * count, model), BF),
            pltpu.VMEM((2 * count, model), F32),
            pltpu.VMEM((model, 2 * count), BF),
            pltpu.VMEM((2 * count, model), BF),
            pltpu.VMEM((model, 2 * count), BF),
            pltpu.VMEM((PARTS - 1, 2 * count, hid), BF),
            pltpu.VMEM((PARTS - 1, 2 * count, hid), F32),
            pltpu.VMEM((PARTS - 1, 2 * count, hid), BF),
            pltpu.VMEM((2 * count, hid), BF),
            pltpu.VMEM((2 * count, model), F32),
            pltpu.VMEM((2 * count, model), BF),
            pltpu.VMEM((2 * count, model), BF),
            pltpu.VMEM((PARTS, chips, shard, hid), F32),
            slots,
            slots,
            slots,
            slots,
            slots,
            pltpu.VMEM((PARTS, shard, hid), BF),
            pltpu.VMEM((2, count, count), BF),
            pltpu.VMEM((3, count, model), BF),
            pltpu.VMEM((2, count, count), BF),
        ]
        + [dma((PARTS, chips))] * 5
        + [dma((PARTS, chips // 2))] * 5
        + [dma((PARTS,))] * 2
        + [dma((4,))] * 3
        + [dma((2,))],
        compiler_params=pltpu.CompilerParams(
            collective_id=0, has_side_effects=True, vmem_limit_bytes=56 * 1024 * 1024
        ),
        cost_estimate=pl.CostEstimate(
            flops=flops,
            bytes_accessed=4 * shard * (proj + hid),
            transcendentals=2 * count * proj,
        ),
    )(acts_fwd, acts_bwd, cotangent, lens_fwd, lens_bwd, w_proj, w_out[0].T)
    next_acts, prev_grads, grad_proj, grad_out = pl.pallas_call(
        finish,
        out_shape=results,
        in_specs=[vmem] * 4,
        out_specs=(vmem,) * 4,
    )(*outs)
    return next_acts, prev_grads, grad_proj, grad_out.T[None]


def solution(mesh):
    return jax.shard_map(
        per_device,
        mesh=mesh,
        in_specs=(
            P("pipe", "dp", None),
            P("pipe", "dp", None),
            P("pipe", "dp", None),
            P("pipe", "dp", None),
            P("pipe", "dp", None),
            P("pipe", "dp", None),
            P("pipe", None, "dp"),
        ),
        out_specs=(
            P("pipe", "dp", None),
            P("pipe", "dp", None),
            P("pipe", "dp", None),
            P("pipe", None, "dp"),
        ),
        check_vma=False,
    )
```

time: 84.8 us -> 68.1 us (0.80)
  Pallas kernels: 84 us -> 67.3 us
    pallas_call x1, Pallas kernels: 81.5 us -> 64.9 us  [per_device(): pl.pallas_call(functools.partial(kernel, chips, phases), out_shape=result...]
where the time goes in v4:
time: 68.1 us; the launch traced here: 68 us
  Pallas kernels  67.3 us (99%)
    pallas_call x1, Pallas kernels, per_device(): pl.pallas_call(functools.partial(kernel, chips, phases), out_shape=result...  64.9 us
    pallas_call x1, Pallas kernels, per_device(): pl.pallas_call(finish, out_shape=results, in_specs=[vmem] * 4, out_specs=...  2.44 us

profile of v4, /device:TPU:0, one launch (start us, length us, event | category | flops | bytes accessed | tf_op | source)
XLA Modules:
  0.0 68.0 jit_solution(505534569219497686)
XLA Ops:
  0.6 64.9 %shard_map.102 = (bf16[1,128,768]{2,1,0:T(8,128)(2,1)}, bf16[1,128,768]{2,1,0:T(8,128)(2,1)}, f32[1,96,2048]{2,1,0:T(8,128)}, f32[96,512]{1,0:T(8,128)}) custom-call(bf16[1,128,768]{2,1,0:T(8,128)(2,1)} %xf_ref.1, bf16[1,128,768]{2,1,0:T(8,128)(2,1)} %xb_ref.1, bf16[1,128,768]{2,1,0:T(8,128)(2,1)} %g_ref.1, s32[1,1,4]{2,1,0:T(1,128)} %lf_ref.1, ...), custom_call_target="tpu_custom_call" | custom-call | flops 2013265920 | bytes 983040 | tf_op jit(solution)/shard_map/pallas_call | solution.py:588
  65.5 2.4 %shard_map.103 = (bf16[1,128,768]{2,1,0:T(8,128)(2,1)}, bf16[1,128,768]{2,1,0:T(8,128)(2,1)}, f32[1,96,2048]{2,1,0:T(8,128)}, f32[96,512]{1,0:T(8,128)}) custom-call(bf16[1,128,768]{2,1,0:T(8,128)(2,1)} %get-tuple-element.12.refs_0_, bf16[1,128,768]{2,1,0:T(8,128)(2,1)} %get-tuple-element.13.refs_1_, f32[1,96,2048]{2,1,0:T(8,128)} %get-tuple-element.14.refs_2_, ...), custom_call_target="tpu_custom_call" | custom-call | tf_op jit(solution)/shard_map/pallas_call | solution.py:633

commit v5 on v4

--- a/solution.py
+++ b/solution.py
@@ -81,6 +81,7 @@
     g_both,
     g_t,
     hidden,
+    hidden_f,
     slope,
     gpre,
     gated_b,
@@ -236,16 +237,17 @@
 
     @pl.when(helper)
     def _():
-        to_mate(0).start()
-        to_mate(1).start()
+        to_mate(val).start()
         act_copy(0).start()
         masks[0] = jagged_mask(lb_ref, count).astype(BF)
         masks[1] = jagged_mask(lf_ref, count).astype(BF)
         act_copy(1).start()
-        for i in range(2, PARTS):
-            to_mate(i).start()
+        to_mate(que).start()
+        to_mate(key).start()
+        act_copy(3).start()
+        to_mate(gat).start()
+        to_mate(out).start()
         act_copy(2).start()
-        act_copy(3).start()
 
         for i in (out, gat, val, que, key):
             final_copy(i).wait_recv()
@@ -324,28 +326,48 @@
         def arrivals(i):
             loop(0, chips, lambda j: from_partner(i, j).wait_recv())
 
-        loop(0, PARTS, mate_part)
-
+        def project_bwd(i):
+            value = dot(xnb[...], wall[i])
+            sigma = sigmoid(value)
+            silu = value * sigma
+            hidden[i] = silu.astype(BF)
+            slope[i] = sigma + silu * (1.0 - sigma)
+
+        def project_fwd(i):
+            value = dot(xnf[...], wall[i])
+            hidden_f[i] = (value * sigmoid(value)).astype(BF)
+
+        mate_part(val)
+        g_both[first, :] = g_ref[0]
+        g_t[:, first] = g_ref[0].astype(F32).T.astype(BF)
+        xnf[first, :] = layer_norm(xf_ref[0].astype(F32))[0].astype(BF)
         act_copy(0).wait_recv()
         inverse_mate = prepare(second, mate_acts[0])
         inverse_b = jnp.concatenate([inverse_own, inverse_mate], axis=0)
-        g_both[first, :] = g_ref[0]
-        g_t[:, first] = g_ref[0].astype(F32).T.astype(BF)
-        xnf[first, :] = layer_norm(xf_ref[0].astype(F32))[0].astype(BF)
+        mate_part(que)
+        line(val)
+        mate_part(key)
+        arrivals(val)
+        project_bwd(val)
+        line(que)
         act_copy(1).wait_recv()
         keeps_b = [jagged_mask(lb_ref, count), mate_masks[0].astype(F32)]
-
-        def project(x_ref, i, with_slope):
-            value = dot(x_ref[...], wall[i])
-            sigma = sigmoid(value)
-            silu = value * sigma
-            hidden[i] = silu.astype(BF)
-            if with_slope:
-                slope[i] = sigma + silu * (1.0 - sigma)
+        keeps_f = [jagged_mask(lf_ref, count), mate_masks[1].astype(F32)]
+        arrivals(que)
+        project_bwd(que)
+        act_copy(3).wait_recv()
+        xnf[second, :] = layer_norm(mate_acts[2].astype(F32))[0].astype(BF)
+        line(key)
+        project_fwd(val)
+        mate_part(gat)
+        arrivals(key)
+        project_bwd(key)
+        project_fwd(que)
+        mate_part(out)
 
         heads = [slice(head * HEAD_DIM, (head + 1) * HEAD_DIM) for head in range(HEADS)]
 
-        def attend(keeps):
+        def attend(hidden, keeps):
             sigmas, scores, attns, blocks = [], [], [], []
             for at, keep in zip((first, second), keeps):
                 mixed = []
@@ -451,14 +473,11 @@
             else:
                 gp_ref[0, :, home(i)] = own[i, z]
 
-        loop(0, gat, line)
-        loop(0, gat, arrivals)
-        loop(0, gat, lambda i: project(xnb, i, True))
         line(gat)
-        sigmas, scores, attns, mixed = attend(keeps_b)
+        sigmas, scores, attns, mixed = attend(hidden, keeps_b)
         mixed_n, inverse_o = layer_norm(mixed)
         arrivals(gat)
-        project(xnb, gat, True)
+        project_bwd(gat)
         gate = hidden[gat].astype(F32)
         gated_b[...] = (mixed_n * gate).astype(BF)
         act_copy(2).wait_recv()
@@ -511,13 +530,11 @@
         out_copy(1, False).start()
         conclude(out)
 
-        act_copy(3).wait_recv()
-        xnf[second, :] = layer_norm(mate_acts[2].astype(F32))[0].astype(BF)
-        loop(0, PARTS - 1, lambda i: project(xnf, i, False))
+        project_fwd(key)
+        project_fwd(gat)
         conclude(gat)
-        keeps_f = [jagged_mask(lf_ref, count), mate_masks[1].astype(F32)]
-        mixed_f = attend(keeps_f)[3]
-        gated_f = (layer_norm(mixed_f)[0] * hidden[gat].astype(F32)).astype(BF)
+        mixed_f = attend(hidden_f, keeps_f)[3]
+        gated_f = (layer_norm(mixed_f)[0] * hidden_f[gat].astype(F32)).astype(BF)
         conclude(val)
         change = dot(gated_f, wall[out], NT)
         fwd_out[second, :] = (mate_acts[2].astype(F32) + change[second]).astype(BF)
@@ -563,9 +580,26 @@
 
 
 def finish(*refs):
-    half = len(refs) // 2
-    for src, dst in zip(refs[:half], refs[half:]):
-        dst[...] = src[...]
+    sources, targets, held, (ins, outs) = refs[:4], refs[4:8], refs[8:12], refs[12:]
+    pieces = []
+    for source, target, slot in zip(sources, targets, held):
+        step = slot.shape[-2] // 2
+        for start in (0, step):
+            at = (0,) * (len(slot.shape) - 2) + (pl.ds(start, step),)
+            n = len(pieces)
+            pieces.append(
+                (
+                    pltpu.make_async_copy(source.at[at], slot.at[at], ins.at[n]),
+                    pltpu.make_async_copy(slot.at[at], target.at[at], outs.at[n]),
+                )
+            )
+    for arrive, _ in pieces:
+        arrive.start()
+    for arrive, leave in pieces:
+        arrive.wait()
+        leave.start()
+    for _, leave in pieces:
+        leave.wait()
 
 
 def per_device(acts_fwd, acts_bwd, cotangent, lens_fwd, lens_bwd, w_proj, w_out):
@@ -575,6 +609,7 @@
     _, shard, proj = w_proj.shape
     hid = w_out.shape[1]
     vmem = pl.BlockSpec(memory_space=pltpu.VMEM)
+    hbm = pl.BlockSpec(memory_space=pl.ANY)
     smem = pl.BlockSpec(memory_space=pltpu.SMEM)
     dma = pltpu.SemaphoreType.DMA
     slots = pltpu.VMEM((PARTS, chips, shard, hid), BF)
@@ -598,6 +633,7 @@
             pltpu.VMEM((model, 2 * count), BF),
             pltpu.VMEM((2 * count, model), BF),
             pltpu.VMEM((model, 2 * count), BF),
+            pltpu.VMEM((PARTS - 1, 2 * count, hid), BF),
             pltpu.VMEM((PARTS - 1, 2 * count, hid), BF),
             pltpu.VMEM((PARTS - 1, 2 * count, hid), F32),
             pltpu.VMEM((PARTS - 1, 2 * count, hid), BF),
@@ -633,8 +669,10 @@
     next_acts, prev_grads, grad_proj, grad_out = pl.pallas_call(
         finish,
         out_shape=results,
-        in_specs=[vmem] * 4,
-        out_specs=(vmem,) * 4,
+        in_specs=[hbm] * 4,
+        out_specs=(hbm,) * 4,
+        scratch_shapes=[pltpu.VMEM(result.shape, result.dtype) for result in results]
+        + [dma((8,))] * 2,
     )(*outs)
     return next_acts, prev_grads, grad_proj, grad_out.T[None]
 

time: 68.1 us -> 69 us (1.013)
  Pallas kernels: 67.3 us -> 68.1 us
    pallas_call x1, Pallas kernels: 64.9 us -> 65.9 us  [per_device(): pl.pallas_call(functools.partial(kernel, chips, phases), out_shape=result...]
where the time goes in v5:
time: 69 us; the launch traced here: 68.8 us
  Pallas kernels  68.1 us (99%)
    pallas_call x1, Pallas kernels, per_device(): pl.pallas_call(functools.partial(kernel, chips, phases), out_shape=result...  65.9 us
    pallas_call x1, Pallas kernels, per_device(): pl.pallas_call(finish, out_shape=results, in_specs=[hbm] * 4, out_specs=(...  2.27 us

profile of v5, /device:TPU:0, one launch (start us, length us, event | category | flops | bytes accessed | tf_op | source)
XLA Modules:
  0.0 68.8 jit_solution(6698581500502847324)
XLA Ops:
  0.6 65.9 %shard_map.102 = (bf16[1,128,768]{2,1,0:T(8,128)(2,1)}, bf16[1,128,768]{2,1,0:T(8,128)(2,1)}, f32[1,96,2048]{2,1,0:T(8,128)}, f32[96,512]{1,0:T(8,128)}) custom-call(bf16[1,128,768]{2,1,0:T(8,128)(2,1)} %xf_ref.1, bf16[1,128,768]{2,1,0:T(8,128)(2,1)} %xb_ref.1, bf16[1,128,768]{2,1,0:T(8,128)(2,1)} %g_ref.1, s32[1,1,4]{2,1,0:T(1,128)} %lf_ref.1, ...), custom_call_target="tpu_custom_call" | custom-call | flops 2013265920 | bytes 983040 | tf_op jit(solution)/shard_map/pallas_call | solution.py:623
  66.5 2.3 %shard_map.103 = (bf16[1,128,768]{2,1,0:T(8,128)(2,1)}, bf16[1,128,768]{2,1,0:T(8,128)(2,1)}, f32[1,96,2048]{2,1,0:T(8,128)}, f32[96,512]{1,0:T(8,128)}) custom-call(bf16[1,128,768]{2,1,0:T(8,128)(2,1)} %get-tuple-element.12.refs_0_, bf16[1,128,768]{2,1,0:T(8,128)(2,1)} %get-tuple-element.13.refs_1_, f32[1,96,2048]{2,1,0:T(8,128)} %get-tuple-element.14.refs_2_, ...), custom_call_target="tpu_custom_call" | custom-call | tf_op jit(solution)/shard_map/pallas_call | solution.py:669

commit v6 on v5

--- a/solution.py
+++ b/solution.py
@@ -78,8 +78,10 @@
     xnb,
     normed_ref,
     norm_t,
+    norm_s,
     g_both,
     g_t,
+    g_s,
     hidden,
     hidden_f,
     slope,
@@ -244,10 +246,10 @@
         act_copy(1).start()
         to_mate(que).start()
         to_mate(key).start()
-        act_copy(3).start()
         to_mate(gat).start()
         to_mate(out).start()
         act_copy(2).start()
+        act_copy(3).start()
 
         for i in (out, gat, val, que, key):
             final_copy(i).wait_recv()
@@ -336,6 +338,12 @@
         def project_fwd(i):
             value = dot(xnf[...], wall[i])
             hidden_f[i] = (value * sigmoid(value)).astype(BF)
+
+        def sort_rows(by_row, sorted_ref):
+            for d in range(chips):
+                at = pl.ds(d * shard, shard)
+                sorted_ref[0, at, :] = by_row[rows(d, c), :]
+                sorted_ref[1, at, :] = by_row[rows(d, 1 - c), :]
 
         mate_part(val)
         g_both[first, :] = g_ref[0]
@@ -355,15 +363,12 @@
         keeps_f = [jagged_mask(lf_ref, count), mate_masks[1].astype(F32)]
         arrivals(que)
         project_bwd(que)
-        act_copy(3).wait_recv()
-        xnf[second, :] = layer_norm(mate_acts[2].astype(F32))[0].astype(BF)
+        mate_part(gat)
         line(key)
-        project_fwd(val)
-        mate_part(gat)
+        sort_rows(norm_t, norm_s)
+        mate_part(out)
         arrivals(key)
         project_bwd(key)
-        project_fwd(que)
-        mate_part(out)
 
         heads = [slice(head * HEAD_DIM, (head + 1) * HEAD_DIM) for head in range(HEADS)]
 
@@ -390,42 +395,45 @@
                 psend.at[i, both(j)], precv.at[i, both(j)], rs_part.at[i, j], rs_precv.at[i, j], partner
             )
 
-        def right_copy(i, j):
+        def right_copy(i, d):
             return remote(
-                stage.at[i, both(j)], lrecv.at[i, both(j)], rs_send.at[i, j], rs_lrecv.at[i, j], right
+                stage.at[i, d], lrecv.at[i, d], rs_send.at[i, d], rs_lrecv.at[i, d], right
             )
 
-        def left_copy(i, j):
+        def left_copy(i, d):
             return remote(
-                stage.at[i, both(j)], rrecv.at[i, both(j)], rs_send.at[i, j], rs_rrecv.at[i, j], left
+                stage.at[i, d], rrecv.at[i, d], rs_send.at[i, d], rs_rrecv.at[i, d], left
             )
 
+        def outer_first(j):
+            return (4 * j + 1 - inner(j), inner(j))
+
         def terms(i):
-            sides, factor = (g_t, gated_b[...]) if i == out else (norm_t, gpre[i])
-
-            def term(k):
-                j = jnp.where(2 * m < pairs, pairs - 1 - k, k)
-                for d in (2 * j, 2 * j + 1):
-                    theirs = dot(sides[rows(d, 1 - c), :], factor) * loss_scale
-                    psend[i, d] = theirs.astype(BF)
-                part_copy(i, j).start()
-                for d in (2 * j, 2 * j + 1):
-                    own[i, d] = dot(sides[rows(d, c), :], factor) * loss_scale
-
-            loop(0, pairs, term)
+            sides, factor = (g_s, gated_b[...]) if i == out else (norm_s, gpre[i])
+            whole = (chips, shard, hid)
+            psend[i] = (dot(sides[1], factor) * loss_scale).astype(BF).reshape(whole)
+
+            def pass_pair(k):
+                part_copy(i, jnp.where(2 * m < pairs, pairs - 1 - k, k)).start()
+
+            loop(0, pairs, pass_pair)
+            own[i] = (dot(sides[0], factor) * loss_scale).reshape(whole)
 
         def chip_sum(i, j):
             part_copy(i, j).wait_recv()
-            at = both(j)
-            own[i, at] = own[i, at] + precv[i, at].astype(F32)
-
-        def add_left(i, j):
-            right_copy(i, j).wait_recv()
-            own[i, both(j)] = own[i, both(j)] + lrecv[i, both(j)].astype(F32)
-
-        def add_right(i, j):
-            left_copy(i, j).wait_recv()
-            own[i, both(j)] = own[i, both(j)] + rrecv[i, both(j)].astype(F32)
+
+        def summed(i, d, from_left, from_right):
+            own[i, d] = own[i, d] + precv[i, d].astype(F32)
+
+            @pl.when(from_left)
+            def _():
+                right_copy(i, d).wait_recv()
+                own[i, d] = own[i, d] + lrecv[i, d].astype(F32)
+
+            @pl.when(from_right)
+            def _():
+                left_copy(i, d).wait_recv()
+                own[i, d] = own[i, d] + rrecv[i, d].astype(F32)
 
         def reduce(i):
             def tick(tau):
@@ -433,41 +441,28 @@
                 def _():
                     j = pairs - 1 - tau + m
                     chip_sum(i, j)
-
-                    @pl.when(has_left)
-                    def _():
-                        add_left(i, j)
-
-                    stage[i, both(j)] = own[i, both(j)].astype(BF)
-                    right_copy(i, j).start()
+                    for d in outer_first(j):
+                        summed(i, d, has_left, False)
+                        stage[i, d] = own[i, d].astype(BF)
+                        right_copy(i, d).start()
 
                 @pl.when(has_left & (tau >= pairs - 1 - m))
                 def _():
                     j = tau - (pairs - 1 - m)
                     chip_sum(i, j)
-
-                    @pl.when(has_right)
-                    def _():
-                        add_right(i, j)
-
-                    stage[i, both(j)] = own[i, both(j)].astype(BF)
-                    left_copy(i, j).start()
+                    for d in outer_first(j):
+                        summed(i, d, False, has_right)
+                        stage[i, d] = own[i, d].astype(BF)
+                        left_copy(i, d).start()
 
             loop(0, pairs - 1, tick)
 
         def conclude(i):
             chip_sum(i, m)
-
-            @pl.when(has_left)
-            def _():
-                add_left(i, m)
-
-            @pl.when(has_right)
-            def _():
-                add_right(i, m)
-
+            summed(i, other, has_left, has_right)
             stage[i, other] = own[i, other].astype(BF)
             final_copy(i).start()
+            summed(i, z, has_left, has_right)
             if i == out:
                 go_ref[...] = own[i, z]
             else:
@@ -483,6 +478,7 @@
         act_copy(2).wait_recv()
         g_both[second, :] = mate_acts[1]
         g_t[:, second] = mate_acts[1].astype(F32).T.astype(BF)
+        sort_rows(g_t, g_s)
         terms(out)
         line(out)
         reduce(out)
@@ -530,8 +526,9 @@
         out_copy(1, False).start()
         conclude(out)
 
-        project_fwd(key)
-        project_fwd(gat)
+        act_copy(3).wait_recv()
+        xnf[second, :] = layer_norm(mate_acts[2].astype(F32))[0].astype(BF)
+        loop(0, PARTS - 1, project_fwd)
         conclude(gat)
         mixed_f = attend(hidden_f, keeps_f)[3]
         gated_f = (layer_norm(mixed_f)[0] * hidden_f[gat].astype(F32)).astype(BF)
@@ -569,7 +566,8 @@
 
                 @pl.when(j != m)
                 def _():
-                    right_copy(i, j).wait_send()
+                    right_copy(i, 2 * j).wait_send()
+                    right_copy(i, 2 * j + 1).wait_send()
 
             loop(0, pairs, pair_sends)
 
@@ -631,8 +629,10 @@
             pltpu.VMEM((2 * count, model), BF),
             pltpu.VMEM((2 * count, model), F32),
             pltpu.VMEM((model, 2 * count), BF),
+            pltpu.VMEM((2, model // 2, 2 * count), BF),
             pltpu.VMEM((2 * count, model), BF),
             pltpu.VMEM((model, 2 * count), BF),
+            pltpu.VMEM((2, model // 2, 2 * count), BF),
             pltpu.VMEM((PARTS - 1, 2 * count, hid), BF),
             pltpu.VMEM((PARTS - 1, 2 * count, hid), BF),
             pltpu.VMEM((PARTS - 1, 2 * count, hid), F32),
@@ -652,8 +652,7 @@
             pltpu.VMEM((3, count, model), BF),
             pltpu.VMEM((2, count, count), BF),
         ]
-        + [dma((PARTS, chips))] * 5
-        + [dma((PARTS, chips // 2))] * 5
+        + [dma((PARTS, chips))] * 10
         + [dma((PARTS,))] * 2
         + [dma((4,))] * 3
         + [dma((2,))],

time: 69 us -> 66.9 us (0.970)
  Pallas kernels: 68.1 us -> 66 us
    pallas_call x1, Pallas kernels: 65.9 us -> 63.8 us  [per_device(): pl.pallas_call(functools.partial(kernel, chips, phases), out_shape=result...]
where the time goes in v6:
time: 66.9 us; the launch traced here: 66.7 us
  Pallas kernels  66 us (99%)
    pallas_call x1, Pallas kernels, per_device(): pl.pallas_call(functools.partial(kernel, chips, phases), out_shape=result...  63.8 us
    pallas_call x1, Pallas kernels, per_device(): pl.pallas_call(finish, out_shape=results, in_specs=[hbm] * 4, out_specs=(...  2.27 us

profile of v6, /device:TPU:0, one launch (start us, length us, event | category | flops | bytes accessed | tf_op | source)
XLA Modules:
  0.0 66.7 jit_solution(9734734568897612043)
XLA Ops:
  0.6 63.8 %shard_map.102 = (bf16[1,128,768]{2,1,0:T(8,128)(2,1)}, bf16[1,128,768]{2,1,0:T(8,128)(2,1)}, f32[1,96,2048]{2,1,0:T(8,128)}, f32[96,512]{1,0:T(8,128)}) custom-call(bf16[1,128,768]{2,1,0:T(8,128)(2,1)} %xf_ref.1, bf16[1,128,768]{2,1,0:T(8,128)(2,1)} %xb_ref.1, bf16[1,128,768]{2,1,0:T(8,128)(2,1)} %g_ref.1, s32[1,1,4]{2,1,0:T(1,128)} %lf_ref.1, ...), custom_call_target="tpu_custom_call" | custom-call | flops 2013265920 | bytes 983040 | tf_op jit(solution)/shard_map/pallas_call | solution.py:621
  64.4 2.3 %shard_map.103 = (bf16[1,128,768]{2,1,0:T(8,128)(2,1)}, bf16[1,128,768]{2,1,0:T(8,128)(2,1)}, f32[1,96,2048]{2,1,0:T(8,128)}, f32[96,512]{1,0:T(8,128)}) custom-call(bf16[1,128,768]{2,1,0:T(8,128)(2,1)} %get-tuple-element.12.refs_0_, bf16[1,128,768]{2,1,0:T(8,128)(2,1)} %get-tuple-element.13.refs_1_, f32[1,96,2048]{2,1,0:T(8,128)} %get-tuple-element.14.refs_2_, ...), custom_call_target="tpu_custom_call" | custom-call | tf_op jit(solution)/shard_map/pallas_call | solution.py:668
